TPU v7x, 32 devices: a whole 2x2x4 slice. The times are simulated.
32 devices in a mesh: section: 4 (over y, x), rows: 2 (over core), dp: 4 (over z).
Axes of the slice: x: 2, y: 2, z: 4, core: 2. Of those that a mesh axis runs over, the one named last changes fastest.
Arguments:
- latent: bfloat16 [8, 2, 8, 8, 192], P('dp', None, 'rows'), may hold values from -6 to 6
- enc_weight: bfloat16 [4, 5184, 192], P('section'), may hold values from -0.078125 to 0.078125
- dec_weight: bfloat16 [4, 5184, 192], P('section'), may hold values from -0.078125 to 0.078125
- enc_gain: float32 [4, 192], P('section'), may hold values from 0.1 to 1.9
- dec_gain: float32 [4, 192], P('section'), may hold values from 0.1 to 1.9
- out_grad: bfloat16 [8, 2, 8, 8, 192], P('dp', None, 'rows'), may hold values from -6 to 6
Outputs:
- enc_wgrad: float32 [4, 5184, 192], P('section', ('rows', 'dp'))
- dec_wgrad: float32 [4, 5184, 192], P('section', ('rows', 'dp'))
- enc_ggrad: float32 [4, 192], P('section', ('rows', 'dp'))
- dec_ggrad: float32 [4, 192], P('section', ('rows', 'dp'))
All inputs are finite; a program needn't handle non-finite values.
Results may differ from a plain program's by a relative error of at most 0.028.
Values may be sent and summed in bfloat16 or wider, within the bound.
A program may use at most 128 MiB of HBM per device.

v0:
```python
import math

import jax
import jax.numpy as jnp
from jax import lax
from jax.sharding import PartitionSpec as P

GROUPS = 32


EPSILON = 1e-05


def padded_2(block, sides, width):
    for axis, dim in sides:
        count = lax.axis_size(axis)
        forward = [(i, i + 1) for i in range(count - 1)]
        backward = [(target, source) for source, target in forward]
        low = lax.ppermute(
            lax.slice_in_dim(block, block.shape[dim] - width, None, axis=dim), axis, forward
        )
        high = lax.ppermute(lax.slice_in_dim(block, 0, width, axis=dim), axis, backward)
        block = jnp.concatenate([low, block, high], axis=dim)
    return block


def passed_along(block, axis, distance):
    devices = range(lax.axis_size(axis))
    route = [(i - distance, i) for i in devices if i - distance in devices]
    return lax.ppermute(block, axis, route)


def spread_groups(values, channels):
    return jnp.repeat(values, channels // GROUPS)


def gather_patches(grown_rows):
    frames, padded_rows, columns, channels = grown_rows.shape
    inner_rows = padded_rows - 2
    padded = jnp.pad(grown_rows, ((1, 1), (0, 0), (1, 1), (0, 0)))
    pieces = []
    for lag_frame in range(3):
        for lag_row in range(3):
            for lag_column in range(3):
                pieces.append(
                    padded[
                        lag_frame : lag_frame + frames,
                        lag_row : lag_row + inner_rows,
                        lag_column : lag_column + columns,
                        :,
                    ]
                )
    return jnp.concatenate(pieces, axis=-1).reshape(frames * inner_rows * columns, 27 * channels)


def flipped(weights):
    channels = weights.shape[1]
    blocks = weights.reshape(27, -1, channels)[::-1]
    return jnp.swapaxes(blocks, 1, 2).reshape(-1, blocks.shape[1])


def take_slot(buffer, slot_index):
    return lax.dynamic_index_in_dim(buffer, slot_index, 0, keepdims=False)


def store_slot(buffer, slot_index, valid_now, new_value):
    kept = jnp.where(valid_now, new_value, take_slot(buffer, slot_index))
    return lax.dynamic_update_index_in_dim(buffer, kept, slot_index, 0)


def weight_gradient(grown_all, cotangent_all):
    patches = jax.vmap(gather_patches)(grown_all)
    patches = patches.reshape(-1, patches.shape[-1])
    flat_cot = cotangent_all.reshape(-1, cotangent_all.shape[-1])
    return lax.dot_general(
        patches, flat_cot, (((0,), (0,)), ((), ())), preferred_element_type=jnp.float32
    )


def norm_stats(volume, counted):
    grouped = volume.reshape(-1, GROUPS, volume.shape[-1] // GROUPS)
    totals = lax.psum(jnp.sum(grouped, axis=(0, 2)), "rows")
    centre = totals / counted
    deviation = grouped - centre[None, :, None]
    spread = lax.psum(jnp.sum(deviation * deviation, axis=(0, 2)), "rows") / counted
    return (centre, lax.rsqrt(spread + EPSILON))


def forward_block(volume, gain_vec, weights, counted):
    channels = volume.shape[-1]
    centre, inverse = norm_stats(volume, counted)
    normed = (volume - spread_groups(centre, channels)) * spread_groups(inverse, channels)
    active = jax.nn.silu(normed * gain_vec).astype(jnp.bfloat16)
    grown_act = padded_2(active, (("rows", 1),), 1)
    conv_out = jnp.dot(gather_patches(grown_act), weights, preferred_element_type=jnp.float32)
    return (grown_act, centre, inverse, volume + conv_out.reshape(volume.shape))


def backward_block(volume, gain_vec, reverse_weights, centre, inverse, cotangent, counted):
    channels = volume.shape[-1]
    inverse_full = spread_groups(inverse, channels)
    normed = (volume - spread_groups(centre, channels)) * inverse_full
    zvalue = normed * gain_vec
    cotangent_low = cotangent.astype(jnp.bfloat16)
    grown_cot = padded_2(cotangent_low, (("rows", 1),), 1)
    act_grad = jnp.dot(
        gather_patches(grown_cot), reverse_weights, preferred_element_type=jnp.float32
    ).reshape(volume.shape)
    logistic = jax.nn.sigmoid(zvalue)
    pre_grad = act_grad * logistic * (1.0 + zvalue * (1.0 - logistic))
    hat_grad = pre_grad * gain_vec
    grouped_grad = hat_grad.reshape(-1, GROUPS, channels // GROUPS)
    grouped_hat = normed.reshape(-1, GROUPS, channels // GROUPS)
    first_sum, second_sum = lax.psum(
        (jnp.sum(grouped_grad, axis=(0, 2)), jnp.sum(grouped_grad * grouped_hat, axis=(0, 2))),
        "rows",
    )
    input_grad = inverse_full * (
        hat_grad
        - spread_groups(first_sum / counted, channels)
        - normed * spread_groups(second_sum / counted, channels)
    )
    gain_part = jnp.sum((pre_grad * normed).reshape(-1, channels), axis=0)
    return (cotangent + input_grad, cotangent_low, gain_part)


def on_device(latent, enc_weight, dec_weight, enc_gain, dec_gain, out_grad):
    section_pos = lax.axis_index("section")
    section_count = lax.axis_size("section")
    batches, frames, rows_here, columns, channels = latent.shape
    counted = frames * rows_here * columns * (channels // GROUPS) * lax.axis_size("rows")
    cells_all = batches * lax.axis_size("dp") * frames * rows_here * lax.axis_size("rows") * columns
    loss_scale = 1.0 / math.sqrt(cells_all)
    clock_len = batches + section_count - 1
    last_pos = section_count - 1
    grown_shape = (batches, frames, rows_here + 2, columns, channels)
    enc_inputs = jnp.zeros(latent.shape, jnp.bfloat16)
    enc_tops = jnp.zeros(latent.shape, jnp.bfloat16)
    enc_grown = jnp.zeros(grown_shape, jnp.bfloat16)
    enc_centre = jnp.zeros((batches, GROUPS), jnp.float32)
    enc_inverse = jnp.zeros((batches, GROUPS), jnp.float32)
    arriving = jnp.zeros(latent.shape[1:], jnp.bfloat16)
    for clock_step in range(clock_len):
        micro_index = clock_step - section_pos
        valid_now = (micro_index >= 0) & (micro_index < batches)
        slot_index = jnp.clip(micro_index, 0, batches - 1)
        entering = jnp.where(section_pos == 0, latent[min(clock_step, batches - 1)], arriving)
        grown_act, centre, inverse, result = forward_block(
            entering.astype(jnp.float32), enc_gain[0], enc_weight[0], counted
        )
        leaving = result.astype(jnp.bfloat16)
        enc_inputs = store_slot(enc_inputs, slot_index, valid_now, entering)
        enc_tops = store_slot(enc_tops, slot_index, valid_now, leaving)
        enc_grown = store_slot(enc_grown, slot_index, valid_now, grown_act)
        enc_centre = store_slot(enc_centre, slot_index, valid_now, centre)
        enc_inverse = store_slot(enc_inverse, slot_index, valid_now, inverse)
        if clock_step + 1 < clock_len:
            arriving = passed_along(leaving, "section", 1)
    dec_downs = jnp.zeros(latent.shape, jnp.bfloat16)
    dec_grown = jnp.zeros(grown_shape, jnp.bfloat16)
    dec_centre = jnp.zeros((batches, GROUPS), jnp.float32)
    dec_inverse = jnp.zeros((batches, GROUPS), jnp.float32)
    arriving = jnp.zeros(latent.shape[1:], jnp.bfloat16)
    for clock_step in range(clock_len):
        micro_index = clock_step - (last_pos - section_pos)
        valid_now = (micro_index >= 0) & (micro_index < batches)
        slot_index = jnp.clip(micro_index, 0, batches - 1)
        coming = jnp.where(section_pos == last_pos, take_slot(enc_tops, slot_index), arriving)
        united = coming.astype(jnp.float32) + take_slot(enc_inputs, slot_index).astype(jnp.float32)
        grown_act, centre, inverse, result = forward_block(
            united, dec_gain[0], dec_weight[0], counted
        )
        dec_downs = store_slot(dec_downs, slot_index, valid_now, coming)
        dec_grown = store_slot(dec_grown, slot_index, valid_now, grown_act)
        dec_centre = store_slot(dec_centre, slot_index, valid_now, centre)
        dec_inverse = store_slot(dec_inverse, slot_index, valid_now, inverse)
        if clock_step + 1 < clock_len:
            arriving = passed_along(result.astype(jnp.bfloat16), "section", -1)
    dec_reverse = flipped(dec_weight[0])
    skip_grads = jnp.zeros(latent.shape, jnp.float32)
    dec_cotangents = jnp.zeros(latent.shape, jnp.bfloat16)
    dec_gain_sum = jnp.zeros((channels,), jnp.float32)
    arriving_grad = jnp.zeros(latent.shape[1:], jnp.float32)
    for clock_step in range(clock_len):
        micro_index = clock_step - section_pos
        valid_now = (micro_index >= 0) & (micro_index < batches)
        slot_index = jnp.clip(micro_index, 0, batches - 1)
        seeded = out_grad[min(clock_step, batches - 1)].astype(jnp.float32) * loss_scale
        incoming = jnp.where(valid_now, jnp.where(section_pos == 0, seeded, arriving_grad), 0.0)
        united = take_slot(dec_downs, slot_index).astype(jnp.float32) + take_slot(
            enc_inputs, slot_index
        ).astype(jnp.float32)
        passed, cotangent_low, gain_part = backward_block(
            united,
            dec_gain[0],
            dec_reverse,
            take_slot(dec_centre, slot_index),
            take_slot(dec_inverse, slot_index),
            incoming,
            counted,
        )
        dec_gain_sum = dec_gain_sum + gain_part
        dec_cotangents = store_slot(dec_cotangents, slot_index, valid_now, cotangent_low)
        skip_grads = store_slot(skip_grads, slot_index, valid_now, passed)
        if clock_step + 1 < clock_len:
            arriving_grad = passed_along(passed.astype(jnp.bfloat16), "section", 1).astype(
                passed.dtype
            )
    dec_gradient = weight_gradient(dec_grown, dec_cotangents)
    enc_reverse = flipped(enc_weight[0])
    enc_cotangents = jnp.zeros(latent.shape, jnp.bfloat16)
    enc_gain_sum = jnp.zeros((channels,), jnp.float32)
    arriving_grad = jnp.zeros(latent.shape[1:], jnp.float32)
    for clock_step in range(clock_len):
        micro_index = clock_step - (last_pos - section_pos)
        valid_now = (micro_index >= 0) & (micro_index < batches)
        slot_index = jnp.clip(micro_index, 0, batches - 1)
        skip_here = take_slot(skip_grads, slot_index)
        incoming = jnp.where(
            valid_now, jnp.where(section_pos == last_pos, skip_here, arriving_grad), 0.0
        )
        volume = take_slot(enc_inputs, slot_index).astype(jnp.float32)
        passed, cotangent_low, gain_part = backward_block(
            volume,
            enc_gain[0],
            enc_reverse,
            take_slot(enc_centre, slot_index),
            take_slot(enc_inverse, slot_index),
            incoming,
            counted,
        )
        enc_gain_sum = enc_gain_sum + gain_part
        enc_cotangents = store_slot(enc_cotangents, slot_index, valid_now, cotangent_low)
        leaving_grad = passed + skip_here
        if clock_step + 1 < clock_len:
            arriving_grad = passed_along(leaving_grad.astype(jnp.bfloat16), "section", -1).astype(
                leaving_grad.dtype
            )
    enc_gradient = weight_gradient(enc_grown, enc_cotangents)
    weight_all, gain_all = (
        lax.psum_scatter(
            jnp.stack([enc_gradient, dec_gradient]), ("rows", "dp"), scatter_dimension=1, tiled=True
        ),
        lax.psum_scatter(
            jnp.stack([enc_gain_sum, dec_gain_sum]), ("rows", "dp"), scatter_dimension=1, tiled=True
        ),
    )
    enc_result = weight_all[0:1]
    dec_result = weight_all[1:2]
    enc_gains = gain_all[0:1]
    dec_gains = gain_all[1:2]
    return (enc_result, dec_result, enc_gains, dec_gains)


def solution(mesh):
    in_specs = (
        P("dp", None, "rows", None, None),
        P("section", None, None),
        P("section", None, None),
        P("section", None),
        P("section", None),
        P("dp", None, "rows", None, None),
    )
    out_specs = (
        P("section", ("rows", "dp"), None),
        P("section", ("rows", "dp"), None),
        P("section", ("rows", "dp")),
        P("section", ("rows", "dp")),
    )
    return jax.shard_map(
        on_device, mesh=mesh, in_specs=in_specs, out_specs=out_specs, check_vma=False
    )
```

profile of v0, /device:TPU:0, one launch (start us, length us, event | category | flops | bytes accessed | tf_op | source)
XLA Modules:
  0.0 645.9 jit_solution(15527558492543826588)
XLA Ops:
  12.7 3.3 psum.266
  16.4 2.5 psum.267
  24.1 3.9 copy.342
  29.9 3.9 copy.382
  35.6 4.5 copy.343
  40.1 3.8 copy.383
  49.9 3.2 constant_dynamic-update-slice_fusion.22
  53.1 4.8 collective-permute-start.2
  60.9 3.0 psum.268
  64.3 2.5 psum.269
  77.1 2.6 constant_dynamic-update-slice_fusion.21
  79.7 3.6 collective-permute-start.5
  85.1 2.5 psum.270
  88.0 2.5 psum.271
  100.6 2.6 constant_dynamic-update-slice_fusion.20
  103.2 4.2 collective-permute-start.8
  109.2 2.5 psum.272
  112.1 2.5 psum.273
  116.6 3.0 collective-permute-start.9
  124.6 2.6 constant_dynamic-update-slice_fusion.19
  127.2 4.7 collective-permute-start.11
  133.7 2.5 psum.274
  137.2 2.5 psum.275
  149.7 2.6 fusion.91
  152.5 2.5 psum.276
  155.5 2.5 psum.277
  167.9 2.6 fusion.66
  172.6 5.0 collective-permute-done.16
  177.8 2.5 psum.278
  181.3 2.5 psum.279
  194.0 2.6 fusion.63
  198.7 4.9 collective-permute-done.19
  203.8 2.5 psum.280
  207.2 2.5 psum.281
  225.2 2.6 fusion.60
  229.3 5.2 collective-permute-done.22
  234.8 2.5 psum.282
  238.2 2.5 psum.283
  251.0 3.2 fusion.57
  256.7 3.7 concatenate.368
  263.5 2.5 psum.284
  270.0 3.1 multiply_reduce_fusion.4
  277.1 5.5 collective-permute-start.28
  294.5 3.1 multiply_reduce_fusion.3
  298.1 3.1 all-reduce.30
  301.6 4.8 collective-permute-start.31
  307.5 2.6 collective-permute-start.52
  311.4 3.6 collective-permute-start.32
  322.3 3.1 multiply_reduce_fusion.2
  328.7 5.0 collective-permute-start.34
  344.5 3.1 multiply_reduce_fusion.1
  350.9 3.6 collective-permute-start.37
  364.8 3.1 multiply_reduce_fusion
  381.2 2.7 fusion.167
  388.6 4.8 collective-permute-done.42
  408.3 5.4 collective-permute-done.45
  429.3 4.7 collective-permute-done.48
  438.3 3.7 concatenate.444
  448.2 3.3 all-reduce.23
  456.5 3.0 collective-permute-done.51
  460.2 3.7 pad_maximum_fusion
  475.5 18.0 %all-reduce.22 = f32[2,192]{1,0:T(2,128)S(1)} all-reduce(f32[2,192]{1,0:T(2,128)S(1)} %pad_maximum_fusion.42), channel_id=3, replica_groups=mesh['section'=4,'rows'=2,'dp'=4] {'rows','dp'}, use_global_device_ids=true, to_apply=%region_125.126.clone | all-reduce | flops 384 | bytes 3072
  494.2 141.7 %all-reduce.34.cloned.1.call-done = f32[2,5184,192]{1,2,0:T(8,128)} async-done(((f32[2,5184,192]{1,2,0:T(8,128)}), f32[2,5184,192]{1,2,0:T(8,128)}) %all-reduce.34.cloned.1.call-update) | async-done | bytes 7962640
  635.9 2.7 constant_dynamic-slice_fusion.83
  (770 shorter events, 261.7 us)
Async XLA Ops:
  7.2 628.7 %all-reduce.34.cloned.1.call-start = ((), (), s32[]{:S(2)}) async-start(), calls=%async_computation | async-start | bytes 16121856
  8.0 36.0 %collective-permute-start.26 = (bf16[2,1,8,192]{3,2,0,1:T(8,128)(2,1)S(1)}, bf16[2,1,8,192]{3,2,0,1:T(8,128)(2,1)S(1)}, u32[]{:S(2)}, u32[]{:S(2)}) collective-permute-start(bf16[2,1,8,192]{3,2,0,1:T(8,128)(2,1)S(1)} %get-tuple-element.655), channel_id=1, source_target_pairs={{0,4},{1,5},{2,6},{3,7},{8,12},{9,13},{10,14},{11,15},{16,20},{17,... | collective-permute-start | bytes 18440 | tf_op jit(solution)/shard_map/ppermute | solution.py:19
  10.4 33.6 %collective-permute-start.27 = (bf16[2,1,8,192]{3,2,0,1:T(8,128)(2,1)S(1)}, bf16[2,1,8,192]{3,2,0,1:T(8,128)(2,1)S(1)}, u32[]{:S(2)}, u32[]{:S(2)}) collective-permute-start(bf16[2,1,8,192]{3,2,0,1:T(8,128)(2,1)S(1)} %get-tuple-element.656), channel_id=1, source_target_pairs={{4,0},{5,1},{6,2},{7,3},{12,8},{13,9},{14,10},{15,11},{20,16},{21,... | collective-permute-start | bytes 18440 | tf_op jit(solution)/shard_map/ppermute | solution.py:22
  19.9 25.7 %collective-permute-start = (bf16[2,1,8,192]{3,2,1,0:T(8,128)(2,1)S(1)}, bf16[2,1,8,192]{3,2,1,0:T(8,128)(2,1)S(1)}, u32[]{:S(2)}, u32[]{:S(2)}) collective-permute-start(bf16[2,1,8,192]{3,2,1,0:T(8,128)(2,1)S(1)} %get-tuple-element.693), channel_id=1, source_target_pairs={{0,4},{1,5},{2,6},{3,7},{8,12},{9,13},{10,14},{11,15},{16,20},{17,... | collective-permute-start | bytes 18440 | tf_op jit(solution)/shard_map/ppermute | solution.py:19
  22.1 23.4 %collective-permute-start.1 = (bf16[2,1,8,192]{3,2,1,0:T(8,128)(2,1)S(1)}, bf16[2,1,8,192]{3,2,1,0:T(8,128)(2,1)S(1)}, u32[]{:S(2)}, u32[]{:S(2)}) collective-permute-start(bf16[2,1,8,192]{3,2,1,0:T(8,128)(2,1)S(1)} %get-tuple-element.694), channel_id=1, source_target_pairs={{4,0},{5,1},{6,2},{7,3},{12,8},{13,9},{14,10},{15,11},{20,16},{21,... | collective-permute-start | bytes 18440 | tf_op jit(solution)/shard_map/ppermute | solution.py:22
  53.1 7.5 %collective-permute-start.2 = (bf16[2,4,8,192]{3,2,0,1:T(8,128)(2,1)}, bf16[2,4,8,192]{3,2,0,1:T(8,128)(2,1)}, u32[]{:S(2)}, u32[]{:S(2)}) collective-permute-start(bf16[2,4,8,192]{3,2,0,1:T(8,128)(2,1)} %get-tuple-element.758), channel_id=1, source_target_pairs={{0,8},{8,16},{16,24},{1,9},{9,17},{17,25},{2,10},{10,18},{18,26},{... | collective-permute-start | bytes 73736 | tf_op jit(solution)/shard_map/ppermute | solution.py:30
  67.7 3.6 collective-permute-start.3
  69.9 3.1 collective-permute-start.4
  79.7 5.1 collective-permute-start.5
  91.3 3.5 collective-permute-start.6
  93.4 3.1 collective-permute-start.7
  103.2 5.8 collective-permute-start.8
  115.4 4.4 collective-permute-start.10
  116.6 3.8 collective-permute-start.9
  119.8 19.9 %copy-start.37 = (f32[2,32]{1,0:T(2,128)}, f32[2,32]{1,0:T(2,128)S(1)}, u32[]{:S(2)}) copy-start(f32[2,32]{1,0:T(2,128)S(1)} %dynamic_update_slice.223) | copy-start | bytes 772
  127.2 6.3 collective-permute-start.11
  140.4 3.4 collective-permute-start.12
  142.5 3.1 collective-permute-start.13
  158.7 4.2 collective-permute-start.14
  160.8 3.1 collective-permute-start.15
  167.9 20.1 %copy-start.9 = (bf16[1,2,4,8,192]{4,3,1,2,0:T(8,128)(2,1)S(1)}, bf16[1,2,4,8,192]{4,3,1,2,0:T(8,128)(2,1)}, u32[]{:S(2)}) copy-start(bf16[1,2,4,8,192]{4,3,1,2,0:T(8,128)(2,1)} %fusion.475) | copy-start | bytes 73732
  170.5 7.0 %collective-permute-start.16 = (bf16[2,4,8,192]{3,2,0,1:T(8,128)(2,1)S(1)}, bf16[2,4,8,192]{3,2,0,1:T(8,128)(2,1)S(1)}, u32[]{:S(2)}, u32[]{:S(2)}) collective-permute-start(bf16[2,4,8,192]{3,2,0,1:T(8,128)(2,1)S(1)} %fusion.66), channel_id=1, source_target_pairs={{8,0},{16,8},{24,16},{9,1},{17,9},{25,17},{10,2},{18,10},{26,18},{... | collective-permute-start | bytes 73736 | tf_op jit(solution)/shard_map/ppermute | solution.py:30
  184.6 3.4 collective-permute-start.17
  186.7 3.1 collective-permute-start.18
  196.5 7.0 %collective-permute-start.19 = (bf16[2,4,8,192]{3,2,0,1:T(8,128)(2,1)S(1)}, bf16[2,4,8,192]{3,2,0,1:T(8,128)(2,1)S(1)}, u32[]{:S(2)}, u32[]{:S(2)}) collective-permute-start(bf16[2,4,8,192]{3,2,0,1:T(8,128)(2,1)S(1)} %fusion.63), channel_id=1, source_target_pairs={{8,0},{16,8},{24,16},{9,1},{17,9},{25,17},{10,2},{18,10},{26,18},{... | collective-permute-start | bytes 73736 | tf_op jit(solution)/shard_map/ppermute | solution.py:30
  210.5 10.6 %collective-permute-start.20 = (bf16[2,1,8,192]{3,2,0,1:T(8,128)(2,1)S(1)}, bf16[2,1,8,192]{3,2,0,1:T(8,128)(2,1)S(1)}, u32[]{:S(2)}, u32[]{:S(2)}) collective-permute-start(bf16[2,1,8,192]{3,2,0,1:T(8,128)(2,1)S(1)} %get-tuple-element.665), channel_id=1, source_target_pairs={{0,4},{1,5},{2,6},{3,7},{8,12},{9,13},{10,14},{11,15},{16,20},{17,... | collective-permute-start | bytes 18440 | tf_op jit(solution)/shard_map/ppermute | solution.py:19
  212.6 8.5 %collective-permute-start.21 = (bf16[2,1,8,192]{3,2,0,1:T(8,128)(2,1)S(1)}, bf16[2,1,8,192]{3,2,0,1:T(8,128)(2,1)S(1)}, u32[]{:S(2)}, u32[]{:S(2)}) collective-permute-start(bf16[2,1,8,192]{3,2,0,1:T(8,128)(2,1)S(1)} %get-tuple-element.666), channel_id=1, source_target_pairs={{4,0},{5,1},{6,2},{7,3},{12,8},{13,9},{14,10},{15,11},{20,16},{21,... | collective-permute-start | bytes 18440 | tf_op jit(solution)/shard_map/ppermute | solution.py:22
  227.8 6.7 %collective-permute-start.22 = (bf16[2,4,8,192]{3,2,0,1:T(8,128)(2,1)S(1)}, bf16[2,4,8,192]{3,2,0,1:T(8,128)(2,1)S(1)}, u32[]{:S(2)}, u32[]{:S(2)}) collective-permute-start(bf16[2,4,8,192]{3,2,0,1:T(8,128)(2,1)S(1)} %fusion.60), channel_id=1, source_target_pairs={{8,0},{16,8},{24,16},{9,1},{17,9},{25,17},{10,2},{18,10},{26,18},{... | collective-permute-start | bytes 73736 | tf_op jit(solution)/shard_map/ppermute | solution.py:30
  241.4 4.2 collective-permute-start.23
  243.6 3.1 collective-permute-start.24
  254.2 7.6 %collective-permute-start.25 = (bf16[2,4,8,192]{3,2,0,1:T(8,128)(2,1)}, bf16[2,4,8,192]{3,2,0,1:T(8,128)(2,1)S(1)}, u32[]{:S(2)}, u32[]{:S(2)}) collective-permute-start(bf16[2,4,8,192]{3,2,0,1:T(8,128)(2,1)} %fusion.57), channel_id=1, source_target_pairs={{8,0},{16,8},{24,16},{9,1},{17,9},{25,17},{10,2},{18,10},{26,18},{... | collective-permute-start | bytes 73736 | tf_op jit(solution)/shard_map/ppermute | solution.py:30
  270.0 18.0 %copy-start.75 = (f32[32]{0:T(128)S(1)}, f32[32]{0:T(128)}, u32[]{:S(2)}) copy-start(f32[32]{0:T(128)} %get-tuple-element.780) | copy-start | bytes 388
  277.1 7.4 %collective-permute-start.28 = (bf16[2,4,8,192]{3,2,0,1:T(8,128)(2,1)}, bf16[2,4,8,192]{3,2,0,1:T(8,128)(2,1)S(1)}, u32[]{:S(2)}, u32[]{:S(2)}) collective-permute-start(bf16[2,4,8,192]{3,2,0,1:T(8,128)(2,1)} %fusion.375), channel_id=1, source_target_pairs={{0,8},{8,16},{16,24},{1,9},{9,17},{17,25},{2,10},{10,18},{18,26},{... | collective-permute-start | bytes 73736 | tf_op jit(solution)/shard_map/ppermute | solution.py:30
  283.6 22.8 %copy-start.3 = (bf16[2,4,8,192]{3,2,1,0:T(8,128)(2,1)}, bf16[2,4,8,192]{3,2,1,0:T(8,128)(2,1)S(1)}, u32[]{:S(2)}) copy-start(bf16[2,4,8,192]{3,2,1,0:T(8,128)(2,1)S(1)} %multiply_convert_fusion) | copy-start | bytes 73732
  284.5 3.7 collective-permute-start.29
  285.8 3.1 collective-permute-start.30
  301.6 9.7 %collective-permute-start.31 = (bf16[2,4,8,192]{3,2,0,1:T(8,128)(2,1)S(1)}, bf16[2,4,8,192]{3,2,0,1:T(8,128)(2,1)S(1)}, u32[]{:S(2)}, u32[]{:S(2)}) collective-permute-start(bf16[2,4,8,192]{3,2,0,1:T(8,128)(2,1)S(1)} %get-tuple-element.64), channel_id=1, source_target_pairs={{0,8},{8,16},{16,24},{1,9},{9,17},{17,25},{2,10},{10,18},{18,26},{... | collective-permute-start | bytes 73736 | tf_op jit(solution)/shard_map/ppermute | solution.py:30
  307.5 108.9 %collective-permute-start.52 = (bf16[2,1,8,192]{3,2,0,1:T(8,128)(2,1)}, bf16[2,1,8,192]{3,2,0,1:T(8,128)(2,1)}, u32[]{:S(2)}, u32[]{:S(2)}) collective-permute-start(bf16[2,1,8,192]{3,2,0,1:T(8,128)(2,1)} %get-tuple-element.657), channel_id=1, source_target_pairs={{0,4},{1,5},{2,6},{3,7},{8,12},{9,13},{10,14},{11,15},{16,20},{17,... | collective-permute-start | bytes 18440 | tf_op jit(solution)/shard_map/ppermute | solution.py:19
  310.0 106.3 %collective-permute-start.53 = (bf16[2,1,8,192]{3,2,1,0:T(8,128)(2,1)}, bf16[2,1,8,192]{3,2,1,0:T(8,128)(2,1)}, u32[]{:S(2)}, u32[]{:S(2)}) collective-permute-start(bf16[2,1,8,192]{3,2,1,0:T(8,128)(2,1)} %get-tuple-element.658), channel_id=1, source_target_pairs={{4,0},{5,1},{6,2},{7,3},{12,8},{13,9},{14,10},{15,11},{20,16},{21,... | collective-permute-start | bytes 18440 | tf_op jit(solution)/shard_map/ppermute | solution.py:22
  311.4 5.1 collective-permute-start.32
  315.0 3.1 collective-permute-start.33
  328.7 6.7 %collective-permute-start.34 = (bf16[2,4,8,192]{3,2,0,1:T(8,128)(2,1)S(1)}, bf16[2,4,8,192]{3,2,0,1:T(8,128)(2,1)S(1)}, u32[]{:S(2)}, u32[]{:S(2)}) collective-permute-start(bf16[2,4,8,192]{3,2,0,1:T(8,128)(2,1)S(1)} %get-tuple-element.62), channel_id=1, source_target_pairs={{0,8},{8,16},{16,24},{1,9},{9,17},{17,25},{2,10},{10,18},{18,26},{... | collective-permute-start | bytes 73736 | tf_op jit(solution)/shard_map/ppermute | solution.py:30
  335.4 3.1 collective-permute-start.35
  337.2 3.1 collective-permute-start.36
  350.9 5.2 collective-permute-start.37
  356.2 2.6 collective-permute-start.38
  357.5 3.1 collective-permute-start.39
  371.9 3.4 collective-permute-start.40
  374.0 3.1 collective-permute-start.41
  383.9 18.0 %copy-start.63 = (f32[192]{0:T(256)S(1)}, f32[192]{0:T(256)}, u32[]{:S(2)}) copy-start(f32[192]{0:T(256)} %mul.956) | copy-start | bytes 2308
  387.3 6.1 collective-permute-start.42
  393.4 2.6 collective-permute-start.43
  394.7 3.1 collective-permute-start.44
  403.6 18.6 %copy-start.61 = (f32[192]{0:T(256)S(1)}, f32[192]{0:T(256)}, u32[]{:S(2)}) copy-start(f32[192]{0:T(256)} %mul.969) | copy-start | bytes 2308
  403.6 18.6 %copy-start.62 = (f32[192]{0:T(256)S(1)}, f32[192]{0:T(256)}, u32[]{:S(2)}) copy-start(f32[192]{0:T(256)} %sub.587) | copy-start | bytes 2308
  407.0 6.7 %collective-permute-start.45 = (bf16[2,4,8,192]{3,2,0,1:T(8,128)(2,1)S(1)}, bf16[2,4,8,192]{3,2,0,1:T(8,128)(2,1)S(1)}, u32[]{:S(2)}, u32[]{:S(2)}) collective-permute-start(bf16[2,4,8,192]{3,2,0,1:T(8,128)(2,1)S(1)} %fusion.184), channel_id=1, source_target_pairs={{8,0},{16,8},{24,16},{9,1},{17,9},{25,17},{10,2},{18,10},{26,18},{... | collective-permute-start | bytes 73736 | tf_op jit(solution)/shard_map/ppermute | solution.py:30
  413.7 3.4 collective-permute-start.46
  415.0 3.1 collective-permute-start.47
  427.3 6.7 %collective-permute-start.48 = (bf16[2,4,8,192]{3,2,0,1:T(8,128)(2,1)S(1)}, bf16[2,4,8,192]{3,2,0,1:T(8,128)(2,1)S(1)}, u32[]{:S(2)}, u32[]{:S(2)}) collective-permute-start(bf16[2,4,8,192]{3,2,0,1:T(8,128)(2,1)S(1)} %fusion.202), channel_id=1, source_target_pairs={{8,0},{16,8},{24,16},{9,1},{17,9},{25,17},{10,2},{18,10},{26,18},{... | collective-permute-start | bytes 73736 | tf_op jit(solution)/shard_map/ppermute | solution.py:30
  434.7 7.3 %collective-permute-start.49 = (bf16[2,1,8,192]{3,2,0,1:T(8,128)(2,1)S(1)}, bf16[2,1,8,192]{3,2,0,1:T(8,128)(2,1)S(1)}, u32[]{:S(2)}, u32[]{:S(2)}) collective-permute-start(bf16[2,1,8,192]{3,2,0,1:T(8,128)(2,1)S(1)} %get-tuple-element.623), channel_id=1, source_target_pairs={{0,4},{1,5},{2,6},{3,7},{8,12},{9,13},{10,14},{11,15},{16,20},{17,... | collective-permute-start | bytes 18440 | tf_op jit(solution)/shard_map/ppermute | solution.py:19
  435.9 6.0 collective-permute-start.50
  452.7 6.7 %collective-permute-start.51 = (bf16[2,4,8,192]{3,2,1,0:T(8,128)(2,1)S(1)}, bf16[2,4,8,192]{3,2,1,0:T(8,128)(2,1)S(1)}, u32[]{:S(2)}, u32[]{:S(2)}) collective-permute-start(bf16[2,4,8,192]{3,2,1,0:T(8,128)(2,1)S(1)} %fusion.224), channel_id=1, source_target_pairs={{8,0},{16,8},{24,16},{9,1},{17,9},{25,17},{10,2},{18,10},{26,18},{... | collective-permute-start | bytes 73736 | tf_op jit(solution)/shard_map/ppermute | solution.py:30
  466.7 2.7 collective-permute-start.54
  468.1 3.1 collective-permute-start.55
  (83 other events, 614.5 us)
Sparse Core Ops, SparseCore 0:
  464.1 171.7 all-reduce.33
where the time goes:
time: 659 us; the launch traced here: 646 us
  waiting for transfers between devices  202 us (31%)
  local copies, waits for them, and re-layouts  129 us (20%)
  starting transfers between devices  114 us (17%)
  blocking collectives  92.4 us (14%)
  matrix products  52.3 us (8%)
  other arithmetic  37.9 us (6%)
  between operations  19 us (3%)
    unnamed x2, waiting for transfers between devices  142 us
    ppermute x16, starting transfers between devices, passed_along(): return lax.ppermute(block, axis, route)  47 us
    concatenate x21, local copies, waits for them, and re-layouts, gather_patches(): jnp.concatenate(pieces, axis=-1)  44.5 us
    ppermute x20, starting transfers between devices, padded_2(): lax.ppermute(lax.slice_in_dim(block, block.shape[dim] - width, None, axis...  40.3 us
    ppermute x16, waiting for transfers between devices, passed_along(): return lax.ppermute(block, axis, route)  38.9 us
    slice x42, local copies, waits for them, and re-layouts, gather_patches(): padded[lag_frame:lag_frame + frames, lag_row:lag_row + inner_rows, lag_co...  31 us
    ppermute x20, starting transfers between devices, padded_2(): lax.ppermute(lax.slice_in_dim(block, 0, width, axis=dim), axis, backward)  26.2 us
    psum x10, blocking collectives, norm_stats(): totals = lax.psum(jnp.sum(grouped, axis=(0, 2)), 'rows')  26 us
  transfers between devices with their start and end apart: 57, of which 28 were waited for; matrix products, arithmetic and copies ran while one was open for 16% of the time, Pallas kernels for 0%

commit v1 on v0

--- a/solution.py
+++ b/solution.py
@@ -1,8 +1,12 @@
+import functools
 import math
 
 import jax
 import jax.numpy as jnp
+import numpy as np
 from jax import lax
+from jax.experimental import pallas as pl
+from jax.experimental.pallas import tpu as pltpu
 from jax.sharding import PartitionSpec as P
 
 GROUPS = 32
@@ -251,6 +255,458 @@
     dec_gains = gain_all[1:2]
     return (enc_result, dec_result, enc_gains, dec_gains)
 
+MESH = pl.DeviceIdType.MESH
+F32, BF16 = jnp.float32, jnp.bfloat16
+
+
+def level_kernel(
+    dims, counted, loss_scale, blocks,
+    lat, grad, we_hbm, wd_hbm, ge, gd, group_ref,
+    out_we, out_wd, out_ge, out_gd,
+    we, wd, we_rev, wd_rev, patch, lat_cells, grad_cells,
+    hin, din, ein, fin, hout, dout, eout, fout, yin,
+    xhat_e, xhat_d, slope_e, slope_d, ga_s, skip, rstd_e, rstd_d,
+    acts_e, acts_d, cots_e, cots_d, gains, vt_e, vt_d, gradient,
+    w_sem, hop_send, hop_recv, half_send, half_recv, all_send, all_recv,
+):
+    ns, nr, nd = dims
+    channels = ge.shape[1]
+    per_row = 16
+    cells = hin.shape[0]
+    half = cells // 2
+    s, r, d = (lax.axis_index(a) for a in ("section", "rows", "dp"))
+    last = ns - 1
+    peers = nr * nd
+    me = r * nd + d
+
+    def peer_id(k):
+        p = lax.rem(me + k, peers)
+        return (s, lax.div(p, nd), lax.rem(p, nd))
+
+    def weight_copies(which):
+        hbm, buf = ((we_hbm, we), (wd_hbm, wd))[which]
+        span = 3 * channels
+        return [
+            pltpu.make_async_copy(
+                hbm.at[dt, dh], buf.at[dh, pl.ds(dt * span, span)], w_sem.at[which, dt * 3 + dh]
+            )
+            for dt in range(3)
+            for dh in range(3)
+        ]
+
+    for which in range(2):
+        for c in weight_copies(which):
+            c.start()
+
+    barrier = pltpu.get_barrier_semaphore()
+    for k in range(1, peers):
+        pl.semaphore_signal(barrier, inc=1, device_id=peer_id(k), device_id_type=MESH)
+
+    @pl.when(s > 0)
+    def _():
+        pl.semaphore_signal(barrier, inc=1, device_id=(s - 1, r, d), device_id_type=MESH)
+
+    @pl.when(s < last)
+    def _():
+        pl.semaphore_signal(barrier, inc=1, device_id=(s + 1, r, d), device_id_type=MESH)
+
+    def by_rows(ref):
+        x = ref[...].astype(F32)
+        x = jnp.stack([x[:, 0], x[:, 1]], axis=2)
+        return x.reshape(2, half, channels).astype(BF16)
+
+    patch[0:per_row, :] = jnp.zeros((per_row, patch.shape[1]), BF16)
+    patch[cells + per_row :, :] = jnp.zeros((per_row, patch.shape[1]), BF16)
+
+    lat_cells[...] = by_rows(lat)
+    grad_cells[...] = by_rows(grad)
+    pl.semaphore_wait(barrier, peers - 1 + (s > 0).astype(jnp.int32) + (s < last).astype(jnp.int32))
+
+    def half_copy(i):
+        source, target = ((lat_cells, hin), (grad_cells, yin))[i]
+        return pltpu.make_async_remote_copy(
+            src_ref=source.at[1 - r],
+            dst_ref=target.at[pl.ds(pl.multiple_of(r * half, half), half)],
+            send_sem=half_send.at[i],
+            recv_sem=half_recv.at[i],
+            device_id=(s, 1 - r, d),
+            device_id_type=MESH,
+        )
+
+    @pl.when(s == 0)
+    def _():
+        half_copy(0).start()
+        half_copy(1).start()
+        mine = pl.ds(pl.multiple_of(r * half, half), half)
+        hin[mine, :] = lat_cells[r]
+        yin[mine, :] = grad_cells[r]
+        half_copy(0).wait()
+
+    def hop(i, step):
+        source, target = ((hout, hin), (dout, din), (eout, ein), (fout, fin))[i]
+        return pltpu.make_async_remote_copy(
+            src_ref=source,
+            dst_ref=target,
+            send_sem=hop_send.at[i],
+            recv_sem=hop_recv.at[i],
+            device_id=(lax.rem(s + step + ns, ns), r, d),
+            device_id_type=MESH,
+        )
+
+    def spread_copy(kind, k, owner):
+        buf = (acts_e, acts_d, cots_d, cots_e, gains)[kind]
+        return pltpu.make_async_remote_copy(
+            src_ref=buf.at[me],
+            dst_ref=buf.at[owner],
+            send_sem=all_send.at[kind, k],
+            recv_sem=all_recv.at[kind, k],
+            device_id=peer_id(k),
+            device_id_type=MESH,
+        )
+
+    def spread_start(kind):
+        for k in range(1, peers):
+            spread_copy(kind, k, me).start()
+
+    def spread_wait(kind):
+        for k in range(1, peers):
+            c = spread_copy(kind, k, lax.rem(me - k + peers, peers))
+            c.wait_send()
+            c.wait_recv()
+
+    row_at = lax.broadcasted_iota(jnp.int32, (16, channels), 0)
+
+    def group_sums(vectors):
+        stacked = jnp.zeros((16, channels), F32)
+        at = 0
+        for x in vectors:
+            hi = x.astype(BF16).astype(F32)
+            mid = (x - hi).astype(BF16).astype(F32)
+            for part in (hi, mid, x - hi - mid):
+                stacked = jnp.where(row_at == at, part, stacked)
+                at += 1
+        out = jnp.dot(stacked.astype(BF16), group_ref[...], preferred_element_type=F32)
+        return [out[3 * i : 3 * i + 1] + out[3 * i + 1 : 3 * i + 2] + out[3 * i + 2 : 3 * i + 3]
+                for i in range(len(vectors))]
+
+    def cell_sum(x):
+        return jnp.sum(x, axis=0, keepdims=True)
+
+    col_at = lax.broadcasted_iota(jnp.int32, (cells // 8, 8, channels), 1)
+
+    def conv(field, w_ref):
+        v = field.reshape(cells // 8, 8, channels)
+        zero = jnp.zeros_like(v)
+        shifted = (
+            jnp.where(col_at >= 1, pltpu.roll(v, 1, 1), zero),
+            v,
+            jnp.where(col_at <= 6, pltpu.roll(v, 7, 1), zero),
+        )
+        none = jnp.zeros((cells // 16, 1, 8, channels), F32)
+        pieces = []
+        for dt in range(3):
+            for x in shifted:
+                x = x.reshape(cells // 16, 2, 8, channels)
+                if dt == 0:
+                    x = jnp.concatenate([none, x[:, :1]], axis=1)
+                elif dt == 2:
+                    x = jnp.concatenate([x[:, 1:], none], axis=1)
+                pieces.append(x.reshape(cells, channels).astype(BF16))
+        patch[per_row : per_row + cells, :] = jnp.concatenate(pieces, axis=1)
+        total = jnp.zeros((cells, channels), F32)
+        for dh in range(3):
+            total = total + jnp.dot(
+                patch[dh * per_row : dh * per_row + cells, :], w_ref[dh],
+                preferred_element_type=F32,
+            )
+        return total
+
+    def normed(x, gain, xhat_ref, rstd_ref, acts):
+        (mean,) = group_sums([cell_sum(x)])
+        x = x - mean / counted
+        (spread,) = group_sums([cell_sum(x * x)])
+        inverse = lax.rsqrt(spread / counted + EPSILON)
+        xhat = x * inverse
+        z = xhat * gain
+        a = (z * jax.nn.sigmoid(z)).astype(BF16)
+        xhat_ref[...] = xhat
+        rstd_ref[...] = inverse
+        acts[me] = a
+        return a.astype(F32)
+
+    def slope(xhat_ref, gain, slope_ref):
+        z = xhat_ref[...] * gain
+        sg = jax.nn.sigmoid(z)
+        slope_ref[...] = sg * (1.0 + z * (1.0 - sg))
+
+    def reverse_weights():
+        for source, target in ((wd, wd_rev), (we, we_rev)):
+            def turn(j, _, source=source, target=target):
+                dh = lax.div(j, 9)
+                b = lax.rem(j, 9)
+                block = source[dh, pl.ds(pl.multiple_of(b * channels, channels), channels), :]
+                target[2 - dh, pl.ds(pl.multiple_of((8 - b) * channels, channels), channels), :] = (
+                    block.astype(F32).T.astype(BF16)
+                )
+                return 0
+            lax.fori_loop(0, 27, turn, 0)
+
+    share = out_we.shape[1]
+    first_block = lax.div(me * share, channels)
+
+    def shifted_acts(kind):
+        buf, target = ((acts_e, vt_e), (acts_d, vt_d))[kind]
+        cell = lax.broadcasted_iota(jnp.int32, (cells, channels), 0)
+        row, frame, col = cell >> 4, (cell >> 3) & 1, cell & 7
+        rows_all = cells // 16
+
+        for j in range(blocks):
+            b = jnp.minimum(first_block + j, 26)
+            dt, dh, dw = lax.div(b, 9) - 1, lax.rem(lax.div(b, 3), 3) - 1, lax.rem(b, 3) - 1
+            turn = lax.rem(cells - (dh * 16 + dt * 8 + dw), cells)
+            valid = (
+                (row + dh >= 0) & (row + dh < rows_all)
+                & (frame + dt >= 0) & (frame + dt < 2)
+                & (col + dw >= 0) & (col + dw < 8)
+            )
+
+            def one(p, _, j=j, turn=turn, valid=valid):
+                x = pltpu.roll(buf[p].astype(F32), turn, 0)
+                x = jnp.where(valid, x, 0.0).T.astype(BF16)
+                target[j, :, pl.ds(pl.multiple_of(p * cells, cells), cells)] = x
+                return 0
+
+            lax.fori_loop(0, peers, one, 0)
+
+    def weight_grads(kind):
+        cots, vt, out = ((cots_e, vt_e, out_we), (cots_d, vt_d, out_wd))[kind]
+        flat = cots[...].reshape(peers * cells, channels)
+        for j in range(blocks):
+            gradient[j * channels : (j + 1) * channels, :] = jnp.dot(
+                vt[j], flat, preferred_element_type=F32
+            )
+        begin = pl.multiple_of(me * share - first_block * channels, 8)
+        out[0] = gradient[pl.ds(begin, share), :]
+
+    def backward(ga, y, gain, xhat_ref, slope_ref, rstd_ref):
+        gz = ga * slope_ref[...]
+        xhat = xhat_ref[...]
+        gx = gz * gain
+        first, second = group_sums([cell_sum(gx), cell_sum(gx * xhat)])
+        result = y + rstd_ref[...] * (gx - first / counted - xhat * (second / counted))
+        return result, gz * xhat
+
+    @pl.when(s > 0)
+    def _():
+        hop(0, -1).wait_recv()
+
+    for c in weight_copies(0):
+        c.wait()
+    x = hin[...].astype(F32)
+    result = x + conv(normed(x, ge[...], xhat_e, rstd_e, acts_e), we)
+    h = result.astype(BF16)
+
+    @pl.when(s < last)
+    def _():
+        hout[...] = h
+        hop(0, 1).start()
+
+    @pl.when(s == last)
+    def _():
+        din[...] = h
+
+    spread_start(0)
+    for c in weight_copies(1):
+        c.wait()
+
+    def first_idle():
+        slope(xhat_e, ge[...], slope_e)
+        reverse_weights()
+
+    @pl.when(s < last)
+    def _():
+        first_idle()
+
+        @pl.when(s == 0)
+        def _():
+            half_copy(1).wait()
+            y = yin[...].astype(F32) * loss_scale
+            yb = y.astype(BF16)
+            cots_d[me] = yb
+            ga_s[...] = conv(yb.astype(F32), wd_rev)
+            spread_start(2)
+
+        spread_wait(0)
+        shifted_acts(0)
+        hop(0, 1).wait_send()
+        hop(1, 1).wait_recv()
+
+    u = din[...].astype(F32) + hin[...].astype(F32)
+    a = normed(u, gd[...], xhat_d, rstd_d, acts_d)
+
+    @pl.when(s > 0)
+    def _():
+        dout[...] = (u + conv(a, wd)).astype(BF16)
+        hop(1, -1).start()
+
+    slope(xhat_d, gd[...], slope_d)
+
+    @pl.when(s == last)
+    def _():
+        spread_start(1)
+        first_idle()
+        spread_wait(0)
+        shifted_acts(0)
+        spread_wait(1)
+        shifted_acts(1)
+
+    @pl.when(s > 0)
+    def _():
+        hop(2, -1).wait_recv()
+        yb = ein[...]
+        cots_d[me] = yb
+        ga_s[...] = conv(yb.astype(F32), wd_rev)
+        yin[...] = yb
+
+    y = jnp.where(s == 0, loss_scale, 1.0) * yin[...].astype(F32)
+    c, gain_cells = backward(ga_s[...], y, gd[...], xhat_d, slope_d, rstd_d)
+    skip[...] = c
+
+    @pl.when(s < last)
+    def _():
+        eout[...] = c.astype(BF16)
+        hop(2, 1).start()
+        spread_start(1)
+
+    dec_gain_row = cell_sum(gain_cells)
+
+    @pl.when(s > 0)
+    def _():
+        spread_start(2)
+
+    @pl.when(s < last)
+    def _():
+        spread_wait(1)
+        shifted_acts(1)
+        spread_wait(2)
+        weight_grads(1)
+        hop(2, 1).wait_send()
+        hop(3, 1).wait_recv()
+
+    c = skip[...]
+    y = jnp.where(s == last, c, fin[...].astype(F32))
+    yb = y.astype(BF16)
+    cots_e[me] = yb
+    spread_start(3)
+    ga = conv(yb.astype(F32), we_rev)
+    f, gain_cells = backward(ga, y, ge[...], xhat_e, slope_e, rstd_e)
+
+    @pl.when(s > 0)
+    def _():
+        fout[...] = (f + c).astype(BF16)
+        hop(3, -1).start()
+
+    enc_gain_row = cell_sum(gain_cells)
+    at8 = lax.broadcasted_iota(jnp.int32, (8, channels), 0)
+    gains[me] = jnp.where(at8 == 0, enc_gain_row, jnp.where(at8 == 1, dec_gain_row, 0.0))
+    spread_start(4)
+
+    @pl.when(s == last)
+    def _():
+        spread_wait(2)
+        weight_grads(1)
+
+    spread_wait(3)
+    weight_grads(0)
+    spread_wait(4)
+    total = jnp.sum(gains[...], axis=0)
+    width = out_ge.shape[1]
+    piece = total[:, 0:width]
+    for i in range(1, peers):
+        piece = jnp.where(me == i, total[:, i * width : (i + 1) * width], piece)
+    out_ge[...] = piece[0:1]
+    out_gd[...] = piece[1:2]
+
+    @pl.when(s > 0)
+    def _():
+        hop(1, -1).wait_send()
+        hop(3, -1).wait_send()
+
+
+def one_kernel(latent, enc_weight, dec_weight, enc_gain, dec_gain, out_grad):
+    batches, frames, rows_here, columns, channels = latent.shape
+    ns, nr, nd = (lax.axis_size(a) for a in ("section", "rows", "dp"))
+    peers = nr * nd
+    cells = frames * rows_here * nr * columns
+    counted = cells * (channels // GROUPS)
+    loss_scale = 1.0 / math.sqrt(batches * nd * cells)
+    taps = 27 * channels
+    share = taps // peers
+    blocks = max(
+        min((i * share + share - 1) // channels, 26) - i * share // channels + 1
+        for i in range(peers)
+    )
+    owner = np.arange(channels) // (channels // GROUPS)
+    groups = jnp.asarray(owner[:, None] == owner[None, :], BF16)
+    field = pltpu.VMEM((cells, channels), BF16)
+    wide = pltpu.VMEM((cells, channels), F32)
+    weights = pltpu.VMEM((3, 9 * channels, channels), BF16)
+    every = pltpu.VMEM((peers, cells, channels), BF16)
+    vector = pltpu.VMEM((1, channels), F32)
+    vmem = pl.BlockSpec(memory_space=pltpu.VMEM)
+    anywhere = pl.BlockSpec(memory_space=pl.ANY)
+    dma = pltpu.SemaphoreType.DMA
+    split = (3, 3, 3 * channels, channels)
+    flops = 2 * cells * taps * channels * 4 + 4 * share * peers * cells * channels
+    return pl.pallas_call(
+        functools.partial(level_kernel, (ns, nr, nd), float(counted), loss_scale, blocks),
+        out_shape=(
+            jax.ShapeDtypeStruct((1, share, channels), F32),
+            jax.ShapeDtypeStruct((1, share, channels), F32),
+            jax.ShapeDtypeStruct((1, channels // peers), F32),
+            jax.ShapeDtypeStruct((1, channels // peers), F32),
+        ),
+        in_specs=[vmem, vmem, anywhere, anywhere, vmem, vmem, vmem],
+        out_specs=(vmem, vmem, vmem, vmem),
+        scratch_shapes=[
+            weights, weights, weights, weights,
+            pltpu.VMEM((cells + 32, 9 * channels), BF16),
+            pltpu.VMEM((2, cells // 2, channels), BF16),
+            pltpu.VMEM((2, cells // 2, channels), BF16),
+            field, field, field, field, field, field, field, field, field,
+            wide, wide, wide, wide, wide, wide, vector, vector,
+            every, every, every, every,
+            pltpu.VMEM((peers, 8, channels), F32),
+            pltpu.VMEM((blocks, channels, peers * cells), BF16),
+            pltpu.VMEM((blocks, channels, peers * cells), BF16),
+            pltpu.VMEM((blocks * channels, channels), F32),
+            dma((2, 9)), dma((4,)), dma((4,)), dma((2,)), dma((2,)),
+            dma((5, peers)), dma((5, peers)),
+        ],
+        compiler_params=pltpu.CompilerParams(
+            collective_id=0, has_side_effects=True, vmem_limit_bytes=48 * 1024 * 1024
+        ),
+        cost_estimate=pl.CostEstimate(
+            flops=flops, bytes_accessed=4 * taps * channels, transcendentals=4 * cells * channels
+        ),
+    )(
+        latent, out_grad, enc_weight.reshape(split), dec_weight.reshape(split),
+        enc_gain, dec_gain, groups,
+    )
+
+
+def per_device(latent, *rest):
+    batches, frames, rows_here, columns, channels = latent.shape
+    rows, dp = lax.axis_size("rows"), lax.axis_size("dp")
+    taps = 27 * channels
+    fits = (
+        rows == 2 and batches == 2 and frames == 2 and columns == 8 and rows_here % 4 == 0
+        and rows_here * rows * 16 == 128
+        and taps % (8 * rows * dp) == 0 and channels % 64 == 0 and channels % (rows * dp) == 0
+        and lax.axis_size("section") > 1
+    )
+    return (one_kernel if fits else on_device)(latent, *rest)
+
 
 def solution(mesh):
     in_specs = (
@@ -268,5 +724,5 @@
         P("section", ("rows", "dp")),
     )
     return jax.shard_map(
-        on_device, mesh=mesh, in_specs=in_specs, out_specs=out_specs, check_vma=False
-    )
+        per_device, mesh=mesh, in_specs=in_specs, out_specs=out_specs, check_vma=False
+    )

time: 659 us -> 110 us (0.17); the launches traced: 646 us -> 110 us
  waiting for transfers between devices: 202 us -> 0 us
  starting transfers between devices: 114 us -> 0 us
  local copies, waits for them, and re-layouts: 129 us -> 15.6 us
  Pallas kernels: 0 us -> 93.4 us
  blocking collectives: 92.4 us -> 0 us
  matrix products: 52.3 us -> 0 us
  other arithmetic: 37.9 us -> 0 us
  between operations: 19 us -> 0.72 us
    unnamed x2 -> x0, waiting for transfers between devices: 142 us -> none
    ppermute x56 -> x0, starting transfers between devices: 114 us -> none  [the longest x16 47 us: passed_along(): return lax.ppermute(block, axis, route)]
    pallas_call x0 -> x1, Pallas kernels: none -> 93.4 us  [one_kernel(): pl.pallas_call(functools.partial(level_kernel, (ns, nr, nd), float(counte...]
    psum x29 -> x0, blocking collectives: 74.4 us -> none  [the longest x10 26 us: norm_stats(): totals = lax.psum(jnp.sum(grouped, axis=(0, 2)), 'rows')]
    ppermute x56 -> x0, waiting for transfers between devices: 60.2 us -> none  [the longest x16 38.9 us: passed_along(): return lax.ppermute(block, axis, route)]
    dot_general x21 -> x0, matrix products: 52.3 us -> none  [the longest x10 25.1 us: backward_block(): jnp.dot(gather_patches(grown_cot), reverse_weights, preferred_element_typ...]
    concatenate x21 -> x0, local copies, waits for them, and re-layouts: 44.5 us -> none  [gather_patches(): jnp.concatenate(pieces, axis=-1)]
    slice x65 -> x0, local copies, waits for them, and re-layouts: 35.9 us -> none  [the longest x42 31 us: gather_patches(): padded[lag_frame:lag_frame + frames, lag_row:lag_row + inner_rows, lag_co...]
  transfers between devices with their start and end apart: 57 -> 0, of which waited for: 28 -> 0; matrix products, arithmetic and copies ran while one was open for 16% -> 0% of each run, Pallas kernels for 0% -> 0%
where the time goes in v1:
time: 110 us
  Pallas kernels  93.4 us (85%)
  local copies, waits for them, and re-layouts  15.6 us (14%)
    pallas_call x1, Pallas kernels, one_kernel(): pl.pallas_call(functools.partial(level_kernel, (ns, nr, nd), float(counte...  93.4 us
    unnamed x20, local copies, waits for them, and re-layouts  12.4 us
    pallas_call x2, local copies, waits for them, and re-layouts, one_kernel(): pl.pallas_call(functools.partial(level_kernel, (ns, nr, nd), float(counte...  3.22 us

profile of v1, /device:TPU:0, one launch (start us, length us, event | category | flops | bytes accessed | tf_op | source)
XLA Modules:
  0.0 109.8 jit_solution(14423296934533642281)
XLA Ops:
  0.6 3.9 %copy.11 = bf16[1,5184,192]{2,1,0:T(8,128)(2,1)S(1)} copy(bf16[1,5184,192]{1,2,0:T(8,128)(2,1)} %param.8) | data formatting | bytes 3981312 | tf_op args[1]
  4.5 0.0 copy-start.1
  4.5 0.0 copy-start.2
  4.5 0.0 copy-start.3
  4.5 0.0 copy-start.4
  4.5 0.0 copy-start.5
  4.6 4.4 %copy.12 = bf16[1,5184,192]{2,1,0:T(8,128)(2,1)} copy(bf16[1,5184,192]{1,2,0:T(8,128)(2,1)} %param.9) | data formatting | bytes 3981312 | tf_op args[2]
  8.9 0.0 copy-done.1
  8.9 0.0 copy-done.2
  8.9 0.0 copy-done.3
  8.9 0.0 copy-done.4
  8.9 0.0 copy-done.5
  8.9 93.4 %shard_map.102 = (f32[1,648,192]{2,1,0:T(8,128)S(1)}, f32[1,648,192]{2,1,0:T(8,128)S(1)}, f32[1,24]{1,0:T(1,128)S(1)}, f32[1,24]{1,0:T(1,128)S(1)}) custom-call(bf16[2,2,4,8,192]{4,3,2,1,0:T(8,128)(2,1)S(1)} %copy-done.1, bf16[2,2,4,8,192]{4,3,2,1,0:T(8,128)(2,1)S(1)} %copy-done.2, bf16[3,3,576,192]{3,2,1,0:T(8,128)(2,1)S(1)} %bitcast.2, ...), custom_call_target="tpu_custom_call" | custom-call | flops 1528823808 | bytes 3981312 | tf_op jit(solution)/shard_map/pallas_call | solution.py:661
  102.4 0.0 copy-start
  102.4 0.8 copy-done
  103.2 0.0 copy-start.6
  103.2 0.5 copy-done.6
  103.8 0.0 copy-start.7
  103.8 0.5 copy-done.7
  104.3 2.2 %copy.13 = f32[1,648,192]{1,2,0:T(8,128)} copy(f32[1,648,192]{2,1,0:T(8,128)} %copy-done) | data formatting | bytes 995328 | tf_op jit(solution)/shard_map/pallas_call | solution.py:661
  106.4 1.1 copy.14
  107.5 1.2 %copy.17 = f32[1,24]{1,0:T(1,128)} copy(f32[1,24]{1,0:T(1,128)} %copy-done.7) | data formatting | bytes 192
  108.7 1.1 %copy.18 = f32[1,24]{1,0:T(1,128)} copy(f32[1,24]{1,0:T(1,128)} %copy-done.6) | data formatting | bytes 192
Async XLA Ops:
  4.5 4.4 %copy-start.1 = (bf16[2,2,4,8,192]{4,3,2,1,0:T(8,128)(2,1)S(1)}, bf16[2,2,4,8,192]{4,3,2,1,0:T(8,128)(2,1)}, u32[]{:S(2)}) copy-start(bf16[2,2,4,8,192]{4,3,2,1,0:T(8,128)(2,1)} %lat.1) | copy-start | bytes 147460
  4.5 4.4 %copy-start.2 = (bf16[2,2,4,8,192]{4,3,2,1,0:T(8,128)(2,1)S(1)}, bf16[2,2,4,8,192]{4,3,2,1,0:T(8,128)(2,1)}, u32[]{:S(2)}) copy-start(bf16[2,2,4,8,192]{4,3,2,1,0:T(8,128)(2,1)} %grad.1) | copy-start | bytes 147460
  4.5 4.4 %copy-start.3 = (f32[1,192]{1,0:T(1,128)S(1)}, f32[1,192]{1,0:T(1,128)}, u32[]{:S(2)}) copy-start(f32[1,192]{1,0:T(1,128)} %ge.1) | copy-start | bytes 2308
  4.5 4.4 %copy-start.4 = (f32[1,192]{1,0:T(1,128)S(1)}, f32[1,192]{1,0:T(1,128)}, u32[]{:S(2)}) copy-start(f32[1,192]{1,0:T(1,128)} %gd.1) | copy-start | bytes 2308
  4.5 4.4 %copy-start.5 = (bf16[192,192]{1,0:T(8,128)(2,1)S(1)}, bf16[192,192]{1,0:T(8,128)(2,1)}, u32[]{:S(2)}) copy-start(bf16[192,192]{1,0:T(8,128)(2,1)} %constant.2.clone.group_ref) | copy-start | bytes 221188
  102.4 0.8 copy-start
  103.2 0.5 copy-start.6
  103.8 0.5 copy-start.7

commit v2 on v1

--- a/solution.py
+++ b/solution.py
@@ -263,7 +263,7 @@
     dims, counted, loss_scale, blocks,
     lat, grad, we_hbm, wd_hbm, ge, gd, group_ref,
     out_we, out_wd, out_ge, out_gd,
-    we, wd, we_rev, wd_rev, patch, lat_cells, grad_cells,
+    wt_e, wt_d, we, wd, we_rev, wd_rev, lat_cells, grad_cells,
     hin, din, ein, fin, hout, dout, eout, fout, yin,
     xhat_e, xhat_d, slope_e, slope_d, ga_s, skip, rstd_e, rstd_d,
     acts_e, acts_d, cots_e, cots_d, gains, vt_e, vt_d, gradient,
@@ -271,7 +271,6 @@
 ):
     ns, nr, nd = dims
     channels = ge.shape[1]
-    per_row = 16
     cells = hin.shape[0]
     half = cells // 2
     s, r, d = (lax.axis_index(a) for a in ("section", "rows", "dp"))
@@ -283,20 +282,12 @@
         p = lax.rem(me + k, peers)
         return (s, lax.div(p, nd), lax.rem(p, nd))
 
-    def weight_copies(which):
-        hbm, buf = ((we_hbm, we), (wd_hbm, wd))[which]
-        span = 3 * channels
-        return [
-            pltpu.make_async_copy(
-                hbm.at[dt, dh], buf.at[dh, pl.ds(dt * span, span)], w_sem.at[which, dt * 3 + dh]
-            )
-            for dt in range(3)
-            for dh in range(3)
-        ]
-
-    for which in range(2):
-        for c in weight_copies(which):
-            c.start()
+    def weight_copy(which):
+        hbm, buf = ((we_hbm, wt_e), (wd_hbm, wt_d))[which]
+        return pltpu.make_async_copy(hbm.at[0], buf, w_sem.at[which])
+
+    weight_copy(0).start()
+    weight_copy(1).start()
 
     barrier = pltpu.get_barrier_semaphore()
     for k in range(1, peers):
@@ -314,9 +305,6 @@
         x = ref[...].astype(F32)
         x = jnp.stack([x[:, 0], x[:, 1]], axis=2)
         return x.reshape(2, half, channels).astype(BF16)
-
-    patch[0:per_row, :] = jnp.zeros((per_row, patch.shape[1]), BF16)
-    patch[cells + per_row :, :] = jnp.zeros((per_row, patch.shape[1]), BF16)
 
     lat_cells[...] = by_rows(lat)
     grad_cells[...] = by_rows(grad)
@@ -340,7 +328,6 @@
         mine = pl.ds(pl.multiple_of(r * half, half), half)
         hin[mine, :] = lat_cells[r]
         yin[mine, :] = grad_cells[r]
-        half_copy(0).wait()
 
     def hop(i, step):
         source, target = ((hout, hin), (dout, din), (eout, ein), (fout, fin))[i]
@@ -403,20 +390,26 @@
             jnp.where(col_at <= 6, pltpu.roll(v, 7, 1), zero),
         )
         none = jnp.zeros((cells // 16, 1, 8, channels), F32)
+        edge = jnp.zeros((16, channels), BF16)
         pieces = []
         for dt in range(3):
+            framed = []
             for x in shifted:
                 x = x.reshape(cells // 16, 2, 8, channels)
                 if dt == 0:
                     x = jnp.concatenate([none, x[:, :1]], axis=1)
                 elif dt == 2:
                     x = jnp.concatenate([x[:, 1:], none], axis=1)
-                pieces.append(x.reshape(cells, channels).astype(BF16))
-        patch[per_row : per_row + cells, :] = jnp.concatenate(pieces, axis=1)
+                framed.append(x.reshape(cells, channels).astype(BF16))
+            pieces += [jnp.concatenate([edge, x[: cells - 16]], axis=0) for x in framed]
+            pieces += framed
+            pieces += [jnp.concatenate([x[16:], edge], axis=0) for x in framed]
         total = jnp.zeros((cells, channels), F32)
-        for dh in range(3):
+        for at in range(0, 27, 4):
+            chunk = pieces[at : at + 4]
             total = total + jnp.dot(
-                patch[dh * per_row : dh * per_row + cells, :], w_ref[dh],
+                jnp.concatenate(chunk, axis=1),
+                w_ref[at * channels : (at + len(chunk)) * channels, :],
                 preferred_element_type=F32,
             )
         return total
@@ -439,19 +432,25 @@
         sg = jax.nn.sigmoid(z)
         slope_ref[...] = sg * (1.0 + z * (1.0 - sg))
 
-    def reverse_weights():
-        for source, target in ((wd, wd_rev), (we, we_rev)):
-            def turn(j, _, source=source, target=target):
-                dh = lax.div(j, 9)
-                b = lax.rem(j, 9)
-                block = source[dh, pl.ds(pl.multiple_of(b * channels, channels), channels), :]
-                target[2 - dh, pl.ds(pl.multiple_of((8 - b) * channels, channels), channels), :] = (
-                    block.astype(F32).T.astype(BF16)
-                )
-                return 0
-            lax.fori_loop(0, 27, turn, 0)
-
-    share = out_we.shape[1]
+    def turn_weights(source, target):
+        step = 2 * channels
+        whole = 27 * channels // step
+
+        def turn(j, _):
+            at = pl.ds(pl.multiple_of(j * step, step), step)
+            target[at, :] = source[:, at].astype(F32).T.astype(BF16)
+            return 0
+
+        lax.fori_loop(0, whole, turn, 0)
+        target[whole * step :, :] = source[:, whole * step :].astype(F32).T.astype(BF16)
+
+    def reverse_weights(source, target):
+        for o in range(27):
+            target[(26 - o) * channels : (27 - o) * channels, :] = source[
+                :, o * channels : (o + 1) * channels
+            ]
+
+    share = 27 * channels // peers
     first_block = lax.div(me * share, channels)
 
     def shifted_acts(kind):
@@ -486,7 +485,7 @@
                 vt[j], flat, preferred_element_type=F32
             )
         begin = pl.multiple_of(me * share - first_block * channels, 8)
-        out[0] = gradient[pl.ds(begin, share), :]
+        out[0] = gradient[pl.ds(begin, share), :].T
 
     def backward(ga, y, gain, xhat_ref, slope_ref, rstd_ref):
         gz = ga * slope_ref[...]
@@ -496,12 +495,46 @@
         result = y + rstd_ref[...] * (gx - first / counted - xhat * (second / counted))
         return result, gz * xhat
 
+    def near_copy(j, owner):
+        if j == 0:
+            to = (s, 1 - r, d)
+        else:
+            to = (s, r, lax.rem(d + j, nd))
+        return pltpu.make_async_remote_copy(
+            src_ref=cots_e.at[me],
+            dst_ref=cots_e.at[owner],
+            send_sem=all_send.at[3, j],
+            recv_sem=all_recv.at[3, j],
+            device_id=to,
+            device_id_type=MESH,
+        )
+
+    def relay_copy(j, core):
+        owner = core * nd + lax.rem(d - j + nd, nd)
+        return pltpu.make_async_remote_copy(
+            src_ref=cots_e.at[owner],
+            dst_ref=cots_e.at[owner],
+            send_sem=all_send.at[3, nd - 1 + j],
+            recv_sem=all_recv.at[3, nd - 1 + j],
+            device_id=(s, 1 - r, d),
+            device_id_type=MESH,
+        )
+
+    late = 2 * s >= ns
+
+    weight_copy(0).wait()
+    turn_weights(wt_e, we)
+
     @pl.when(s > 0)
     def _():
+        weight_copy(1).wait()
+        turn_weights(wt_d, wd)
         hop(0, -1).wait_recv()
 
-    for c in weight_copies(0):
-        c.wait()
+    @pl.when(s == 0)
+    def _():
+        half_copy(0).wait()
+
     x = hin[...].astype(F32)
     result = x + conv(normed(x, ge[...], xhat_e, rstd_e, acts_e), we)
     h = result.astype(BF16)
@@ -516,16 +549,15 @@
         din[...] = h
 
     spread_start(0)
-    for c in weight_copies(1):
-        c.wait()
+
+    @pl.when(s == 0)
+    def _():
+        weight_copy(1).wait()
 
     def first_idle():
         slope(xhat_e, ge[...], slope_e)
-        reverse_weights()
-
-    @pl.when(s < last)
-    def _():
-        first_idle()
+        reverse_weights(wt_d, wd_rev)
+        reverse_weights(wt_e, we_rev)
 
         @pl.when(s == 0)
         def _():
@@ -538,6 +570,13 @@
 
         spread_wait(0)
         shifted_acts(0)
+
+    @pl.when(jnp.logical_not(late))
+    def _():
+        first_idle()
+
+    @pl.when(s < last)
+    def _():
         hop(0, 1).wait_send()
         hop(1, 1).wait_recv()
 
@@ -548,15 +587,13 @@
     def _():
         dout[...] = (u + conv(a, wd)).astype(BF16)
         hop(1, -1).start()
+        spread_start(1)
 
     slope(xhat_d, gd[...], slope_d)
 
-    @pl.when(s == last)
-    def _():
-        spread_start(1)
+    @pl.when(late)
+    def _():
         first_idle()
-        spread_wait(0)
-        shifted_acts(0)
         spread_wait(1)
         shifted_acts(1)
 
@@ -576,20 +613,26 @@
     def _():
         eout[...] = c.astype(BF16)
         hop(2, 1).start()
+
+    dec_gain_row = cell_sum(gain_cells)
+
+    @pl.when(s == 0)
+    def _():
         spread_start(1)
 
-    dec_gain_row = cell_sum(gain_cells)
-
     @pl.when(s > 0)
     def _():
         spread_start(2)
 
-    @pl.when(s < last)
+    @pl.when(jnp.logical_not(late))
     def _():
         spread_wait(1)
         shifted_acts(1)
         spread_wait(2)
         weight_grads(1)
+
+    @pl.when(s < last)
+    def _():
         hop(2, 1).wait_send()
         hop(3, 1).wait_recv()
 
@@ -597,7 +640,8 @@
     y = jnp.where(s == last, c, fin[...].astype(F32))
     yb = y.astype(BF16)
     cots_e[me] = yb
-    spread_start(3)
+    for j in range(nd - 1, -1, -1):
+        near_copy(j, me).start()
     ga = conv(yb.astype(F32), we_rev)
     f, gain_cells = backward(ga, y, ge[...], xhat_e, slope_e, rstd_e)
 
@@ -611,12 +655,18 @@
     gains[me] = jnp.where(at8 == 0, enc_gain_row, jnp.where(at8 == 1, dec_gain_row, 0.0))
     spread_start(4)
 
-    @pl.when(s == last)
+    for j in range(1, nd):
+        near_copy(j, r * nd + lax.rem(d - j + nd, nd)).wait_recv()
+        relay_copy(j, r).start()
+
+    @pl.when(late)
     def _():
         spread_wait(2)
         weight_grads(1)
 
-    spread_wait(3)
+    near_copy(0, (1 - r) * nd + d).wait_recv()
+    for j in range(1, nd):
+        relay_copy(j, 1 - r).wait_recv()
     weight_grads(0)
     spread_wait(4)
     total = jnp.sum(gains[...], axis=0)
@@ -631,6 +681,22 @@
     def _():
         hop(1, -1).wait_send()
         hop(3, -1).wait_send()
+
+    for j in range(nd):
+        near_copy(j, me).wait_send()
+    for j in range(1, nd):
+        relay_copy(j, r).wait_send()
+
+
+def write_kernel(*refs):
+    sources, targets, sems = refs[:4], refs[4:8], refs[8]
+    copies = [
+        pltpu.make_async_copy(a, b, sems.at[i]) for i, (a, b) in enumerate(zip(sources, targets))
+    ]
+    for c in copies:
+        c.start()
+    for c in copies:
+        c.wait()
 
 
 def one_kernel(latent, enc_weight, dec_weight, enc_gain, dec_gain, out_grad):
@@ -650,27 +716,24 @@
     groups = jnp.asarray(owner[:, None] == owner[None, :], BF16)
     field = pltpu.VMEM((cells, channels), BF16)
     wide = pltpu.VMEM((cells, channels), F32)
-    weights = pltpu.VMEM((3, 9 * channels, channels), BF16)
+    weights = pltpu.VMEM((taps, channels), BF16)
+    turned = pltpu.VMEM((channels, taps), BF16)
     every = pltpu.VMEM((peers, cells, channels), BF16)
     vector = pltpu.VMEM((1, channels), F32)
     vmem = pl.BlockSpec(memory_space=pltpu.VMEM)
     anywhere = pl.BlockSpec(memory_space=pl.ANY)
     dma = pltpu.SemaphoreType.DMA
-    split = (3, 3, 3 * channels, channels)
     flops = 2 * cells * taps * channels * 4 + 4 * share * peers * cells * channels
-    return pl.pallas_call(
+    grads = jax.ShapeDtypeStruct((1, channels, share), F32)
+    gain_grads = jax.ShapeDtypeStruct((1, channels // peers), F32)
+    shapes = (grads, grads, gain_grads, gain_grads)
+    results = pl.pallas_call(
         functools.partial(level_kernel, (ns, nr, nd), float(counted), loss_scale, blocks),
-        out_shape=(
-            jax.ShapeDtypeStruct((1, share, channels), F32),
-            jax.ShapeDtypeStruct((1, share, channels), F32),
-            jax.ShapeDtypeStruct((1, channels // peers), F32),
-            jax.ShapeDtypeStruct((1, channels // peers), F32),
-        ),
+        out_shape=shapes,
         in_specs=[vmem, vmem, anywhere, anywhere, vmem, vmem, vmem],
         out_specs=(vmem, vmem, vmem, vmem),
         scratch_shapes=[
-            weights, weights, weights, weights,
-            pltpu.VMEM((cells + 32, 9 * channels), BF16),
+            turned, turned, weights, weights, weights, weights,
             pltpu.VMEM((2, cells // 2, channels), BF16),
             pltpu.VMEM((2, cells // 2, channels), BF16),
             field, field, field, field, field, field, field, field, field,
@@ -680,7 +743,7 @@
             pltpu.VMEM((blocks, channels, peers * cells), BF16),
             pltpu.VMEM((blocks, channels, peers * cells), BF16),
             pltpu.VMEM((blocks * channels, channels), F32),
-            dma((2, 9)), dma((4,)), dma((4,)), dma((2,)), dma((2,)),
+            dma((2,)), dma((4,)), dma((4,)), dma((2,)), dma((2,)),
             dma((5, peers)), dma((5, peers)),
         ],
         compiler_params=pltpu.CompilerParams(
@@ -690,9 +753,17 @@
             flops=flops, bytes_accessed=4 * taps * channels, transcendentals=4 * cells * channels
         ),
     )(
-        latent, out_grad, enc_weight.reshape(split), dec_weight.reshape(split),
+        latent, out_grad, jnp.swapaxes(enc_weight, 1, 2), jnp.swapaxes(dec_weight, 1, 2),
         enc_gain, dec_gain, groups,
     )
+    enc, dec, enc_g, dec_g = pl.pallas_call(
+        write_kernel,
+        out_shape=shapes,
+        in_specs=[vmem] * 4,
+        out_specs=(anywhere,) * 4,
+        scratch_shapes=[dma((4,))],
+    )(*results)
+    return (jnp.swapaxes(enc, 1, 2), jnp.swapaxes(dec, 1, 2), enc_g, dec_g)
 
 
 def per_device(latent, *rest):

time: 110 us -> 86.1 us (0.78); the launches traced: 110 us -> 84.7 us
  Pallas kernels: 93.4 us -> 74.3 us
  local copies, waits for them, and re-layouts: 15.6 us -> 9.73 us
    pallas_call x1, Pallas kernels: 93.4 us -> 72 us  [one_kernel(): pl.pallas_call(functools.partial(level_kernel, (ns, nr, nd), float(counte...]
    pallas_call x2 -> x0, local copies, waits for them, and re-layouts: 3.22 us -> none  [one_kernel(): pl.pallas_call(functools.partial(level_kernel, (ns, nr, nd), float(counte...]
    unnamed x20 -> x22, local copies, waits for them, and re-layouts: 12.4 us -> 9.73 us
    pallas_call x0 -> x1, Pallas kernels: none -> 2.29 us  [one_kernel(): pl.pallas_call(write_kernel, out_shape=shapes, in_specs=[vmem] * 4, out_s...]
where the time goes in v2:
time: 86.1 us; the launch traced here: 84.7 us
  Pallas kernels  74.3 us (86%)
  local copies, waits for them, and re-layouts  9.73 us (11%)
    pallas_call x1, Pallas kernels, one_kernel(): pl.pallas_call(functools.partial(level_kernel, (ns, nr, nd), float(counte...  72 us
    unnamed x22, local copies, waits for them, and re-layouts  9.73 us
    pallas_call x1, Pallas kernels, one_kernel(): pl.pallas_call(write_kernel, out_shape=shapes, in_specs=[vmem] * 4, out_s...  2.29 us

profile of v2, /device:TPU:0, one launch (start us, length us, event | category | flops | bytes accessed | tf_op | source)
XLA Modules:
  0.0 84.7 jit_solution(11921734903072135637)
XLA Ops:
  0.6 0.0 copy-start.4
  0.6 1.6 %copy-done.4 = bf16[1,5184,192]{1,2,0:T(8,128)(2,1)S(1)} copy-done((bf16[1,5184,192]{1,2,0:T(8,128)(2,1)S(1)}, bf16[1,5184,192]{1,2,0:T(8,128)(2,1)}, u32[]{:S(2)}) %copy-start.4) | copy-done | bytes 1990680
  2.2 0.0 copy-start.5
  2.2 1.6 %copy-done.5 = bf16[1,5184,192]{1,2,0:T(8,128)(2,1)S(1)} copy-done((bf16[1,5184,192]{1,2,0:T(8,128)(2,1)S(1)}, bf16[1,5184,192]{1,2,0:T(8,128)(2,1)}, u32[]{:S(2)}) %copy-start.5) | copy-done | bytes 1990680
  3.8 0.0 copy-start.6
  3.8 0.8 copy-done.6
  4.6 0.0 copy-start.7
  4.6 0.8 copy-done.7
  5.4 0.0 copy-start.8
  5.4 0.7 copy-done.8
  6.1 0.0 copy-start.9
  6.1 0.7 copy-done.9
  6.8 0.0 copy-start.10
  6.8 0.9 %copy-done.10 = bf16[192,192]{1,0:T(8,128)(2,1)S(1)} copy-done((bf16[192,192]{1,0:T(8,128)(2,1)S(1)}, bf16[192,192]{1,0:T(8,128)(2,1)}, u32[]{:S(2)}) %copy-start.10) | copy-done | bytes 73752
  7.7 72.0 %shard_map.102 = (f32[1,192,648]{2,1,0:T(8,128)S(1)}, f32[1,192,648]{2,1,0:T(8,128)S(1)}, f32[1,24]{1,0:T(1,128)S(1)}, f32[1,24]{1,0:T(1,128)S(1)}) custom-call(bf16[2,2,4,8,192]{4,3,2,1,0:T(8,128)(2,1)S(1)} %copy-done.6, bf16[2,2,4,8,192]{4,3,2,1,0:T(8,128)(2,1)S(1)} %copy-done.7, bf16[1,192,5184]{2,1,0:T(8,128)(2,1)S(1)} %bitcast.4, ...), custom_call_target="tpu_custom_call" | custom-call | flops 1528823808 | bytes 3981312 | tf_op jit(solution)/shard_map/pallas_call | solution.py:730
  79.7 0.0 copy-start
  79.7 0.8 copy-done
  80.6 0.0 copy-start.1
  80.6 0.8 copy-done.1
  81.4 0.0 copy-start.2
  81.4 0.6 copy-done.2
  81.9 0.0 copy-start.3
  81.9 0.5 copy-done.3
  82.4 2.3 %shard_map.103 = (f32[1,192,648]{2,1,0:T(8,128)}, f32[1,192,648]{2,1,0:T(8,128)}, f32[1,24]{1,0:T(1,128)}, f32[1,24]{1,0:T(1,128)}) custom-call(f32[1,192,648]{2,1,0:T(8,128)} %copy-done, f32[1,192,648]{2,1,0:T(8,128)} %copy-done.1, f32[1,24]{1,0:T(1,128)} %copy-done.2, f32[1,24]{1,0:T(1,128)} %copy-done.3), custom_call_target="tpu_custom_call" | custom-call | tf_op jit(solution)/shard_map/pallas_call | solution.py:759
Async XLA Ops:
  0.6 1.6 %copy-start.4 = (bf16[1,5184,192]{1,2,0:T(8,128)(2,1)S(1)}, bf16[1,5184,192]{1,2,0:T(8,128)(2,1)}, u32[]{:S(2)}) copy-start(bf16[1,5184,192]{1,2,0:T(8,128)(2,1)} %param.8) | copy-start | bytes 5971972
  2.2 1.6 %copy-start.5 = (bf16[1,5184,192]{1,2,0:T(8,128)(2,1)S(1)}, bf16[1,5184,192]{1,2,0:T(8,128)(2,1)}, u32[]{:S(2)}) copy-start(bf16[1,5184,192]{1,2,0:T(8,128)(2,1)} %param.9) | copy-start | bytes 5971972
  3.8 0.8 copy-start.6
  4.6 0.8 copy-start.7
  5.4 0.7 copy-start.8
  6.1 0.7 copy-start.9
  6.8 0.9 %copy-start.10 = (bf16[192,192]{1,0:T(8,128)(2,1)S(1)}, bf16[192,192]{1,0:T(8,128)(2,1)}, u32[]{:S(2)}) copy-start(bf16[192,192]{1,0:T(8,128)(2,1)} %constant.2.clone.group_ref) | copy-start | bytes 221188
  79.7 0.8 copy-start
  80.6 0.8 copy-start.1
  81.4 0.6 copy-start.2
  81.9 0.5 copy-start.3

commit v3 on v2

--- a/solution.py
+++ b/solution.py
@@ -3,7 +3,6 @@
 
 import jax
 import jax.numpy as jnp
-import numpy as np
 from jax import lax
 from jax.experimental import pallas as pl
 from jax.experimental.pallas import tpu as pltpu
@@ -261,13 +260,14 @@
 
 def level_kernel(
     dims, counted, loss_scale, blocks,
-    lat, grad, we_hbm, wd_hbm, ge, gd, group_ref,
+    lat_hbm, grad_hbm, we_hbm, wd_hbm, ge_hbm, gd_hbm,
     out_we, out_wd, out_ge, out_gd,
+    lat, grad, ge, gd, group_ref,
     wt_e, wt_d, we, wd, we_rev, wd_rev, lat_cells, grad_cells,
     hin, din, ein, fin, hout, dout, eout, fout, yin,
     xhat_e, xhat_d, slope_e, slope_d, ga_s, skip, rstd_e, rstd_d,
     acts_e, acts_d, cots_e, cots_d, gains, vt_e, vt_d, gradient,
-    w_sem, hop_send, hop_recv, half_send, half_recv, all_send, all_recv,
+    w_sem, in_sem, hop_send, hop_recv, half_send, half_recv, all_send, all_recv,
 ):
     ns, nr, nd = dims
     channels = ge.shape[1]
@@ -277,10 +277,18 @@
     last = ns - 1
     peers = nr * nd
     me = r * nd + d
+    slot = d * nr + r
 
     def peer_id(k):
-        p = lax.rem(me + k, peers)
-        return (s, lax.div(p, nd), lax.rem(p, nd))
+        p = lax.rem(slot + k, peers)
+        return (s, lax.rem(p, nr), lax.div(p, nr))
+
+    small = [
+        pltpu.make_async_copy(a, b, in_sem.at[i])
+        for i, (a, b) in enumerate(((lat_hbm, lat), (grad_hbm, grad), (ge_hbm, ge), (gd_hbm, gd)))
+    ]
+    small[0].start()
+    small[2].start()
 
     def weight_copy(which):
         hbm, buf = ((we_hbm, wt_e), (wd_hbm, wt_d))[which]
@@ -288,6 +296,8 @@
 
     weight_copy(0).start()
     weight_copy(1).start()
+    small[1].start()
+    small[3].start()
 
     barrier = pltpu.get_barrier_semaphore()
     for k in range(1, peers):
@@ -306,7 +316,18 @@
         x = jnp.stack([x[:, 0], x[:, 1]], axis=2)
         return x.reshape(2, half, channels).astype(BF16)
 
+    size = channels // GROUPS
+    own = [
+        jnp.floor(
+            (lax.broadcasted_iota(jnp.int32, (channels, channels), i).astype(F32) + 0.5) / size
+        )
+        for i in range(2)
+    ]
+    group_ref[...] = jnp.where(own[0] == own[1], 1.0, 0.0).astype(BF16)
+
+    small[0].wait()
     lat_cells[...] = by_rows(lat)
+    small[1].wait()
     grad_cells[...] = by_rows(grad)
     pl.semaphore_wait(barrier, peers - 1 + (s > 0).astype(jnp.int32) + (s < last).astype(jnp.int32))
 
@@ -343,7 +364,7 @@
     def spread_copy(kind, k, owner):
         buf = (acts_e, acts_d, cots_d, cots_e, gains)[kind]
         return pltpu.make_async_remote_copy(
-            src_ref=buf.at[me],
+            src_ref=buf.at[slot],
             dst_ref=buf.at[owner],
             send_sem=all_send.at[kind, k],
             recv_sem=all_recv.at[kind, k],
@@ -353,11 +374,11 @@
 
     def spread_start(kind):
         for k in range(1, peers):
-            spread_copy(kind, k, me).start()
+            spread_copy(kind, k, slot).start()
 
     def spread_wait(kind):
         for k in range(1, peers):
-            c = spread_copy(kind, k, lax.rem(me - k + peers, peers))
+            c = spread_copy(kind, k, lax.rem(slot - k + peers, peers))
             c.wait_send()
             c.wait_recv()
 
@@ -424,7 +445,7 @@
         a = (z * jax.nn.sigmoid(z)).astype(BF16)
         xhat_ref[...] = xhat
         rstd_ref[...] = inverse
-        acts[me] = a
+        acts[slot] = a
         return a.astype(F32)
 
     def slope(xhat_ref, gain, slope_ref):
@@ -477,15 +498,28 @@
 
             lax.fori_loop(0, peers, one, 0)
 
-    def weight_grads(kind):
-        cots, vt, out = ((cots_e, vt_e, out_we), (cots_d, vt_d, out_wd))[kind]
-        flat = cots[...].reshape(peers * cells, channels)
+    pair = nr * cells
+
+    def add_chip(kind, chip, first):
+        cots, vt = ((cots_e, vt_e), (cots_d, vt_d))[kind]
+        at = pl.ds(pl.multiple_of(chip * pair, pair), pair)
+        flat = cots[pl.ds(chip * nr, nr)].reshape(pair, channels)
+        for j in range(blocks):
+            term = jnp.dot(vt[j, :, at], flat, preferred_element_type=F32)
+            rows = slice(j * channels, (j + 1) * channels)
+            gradient[rows, :] = term if first else gradient[rows, :] + term
+
+    def write_grads(out):
+        begin = pl.multiple_of(me * share - first_block * channels, 8)
+        out[0] = gradient[pl.ds(begin, share), :].T
+
+    def dec_weight_grads():
+        flat = cots_d[...].reshape(peers * cells, channels)
         for j in range(blocks):
             gradient[j * channels : (j + 1) * channels, :] = jnp.dot(
-                vt[j], flat, preferred_element_type=F32
+                vt_d[j], flat, preferred_element_type=F32
             )
-        begin = pl.multiple_of(me * share - first_block * channels, 8)
-        out[0] = gradient[pl.ds(begin, share), :].T
+        write_grads(out_wd)
 
     def backward(ga, y, gain, xhat_ref, slope_ref, rstd_ref):
         gz = ga * slope_ref[...]
@@ -501,7 +535,7 @@
         else:
             to = (s, r, lax.rem(d + j, nd))
         return pltpu.make_async_remote_copy(
-            src_ref=cots_e.at[me],
+            src_ref=cots_e.at[slot],
             dst_ref=cots_e.at[owner],
             send_sem=all_send.at[3, j],
             recv_sem=all_recv.at[3, j],
@@ -510,7 +544,7 @@
         )
 
     def relay_copy(j, core):
-        owner = core * nd + lax.rem(d - j + nd, nd)
+        owner = lax.rem(d - j + nd, nd) * nr + core
         return pltpu.make_async_remote_copy(
             src_ref=cots_e.at[owner],
             dst_ref=cots_e.at[owner],
@@ -521,6 +555,8 @@
         )
 
     late = 2 * s >= ns
+    small[2].wait()
+    small[3].wait()
 
     weight_copy(0).wait()
     turn_weights(wt_e, we)
@@ -564,7 +600,7 @@
             half_copy(1).wait()
             y = yin[...].astype(F32) * loss_scale
             yb = y.astype(BF16)
-            cots_d[me] = yb
+            cots_d[slot] = yb
             ga_s[...] = conv(yb.astype(F32), wd_rev)
             spread_start(2)
 
@@ -601,7 +637,7 @@
     def _():
         hop(2, -1).wait_recv()
         yb = ein[...]
-        cots_d[me] = yb
+        cots_d[slot] = yb
         ga_s[...] = conv(yb.astype(F32), wd_rev)
         yin[...] = yb
 
@@ -629,7 +665,7 @@
         spread_wait(1)
         shifted_acts(1)
         spread_wait(2)
-        weight_grads(1)
+        dec_weight_grads()
 
     @pl.when(s < last)
     def _():
@@ -639,9 +675,9 @@
     c = skip[...]
     y = jnp.where(s == last, c, fin[...].astype(F32))
     yb = y.astype(BF16)
-    cots_e[me] = yb
+    cots_e[slot] = yb
     for j in range(nd - 1, -1, -1):
-        near_copy(j, me).start()
+        near_copy(j, slot).start()
     ga = conv(yb.astype(F32), we_rev)
     f, gain_cells = backward(ga, y, ge[...], xhat_e, slope_e, rstd_e)
 
@@ -652,22 +688,24 @@
 
     enc_gain_row = cell_sum(gain_cells)
     at8 = lax.broadcasted_iota(jnp.int32, (8, channels), 0)
-    gains[me] = jnp.where(at8 == 0, enc_gain_row, jnp.where(at8 == 1, dec_gain_row, 0.0))
+    gains[slot] = jnp.where(at8 == 0, enc_gain_row, jnp.where(at8 == 1, dec_gain_row, 0.0))
     spread_start(4)
 
     for j in range(1, nd):
-        near_copy(j, r * nd + lax.rem(d - j + nd, nd)).wait_recv()
+        near_copy(j, lax.rem(d - j + nd, nd) * nr + r).wait_recv()
         relay_copy(j, r).start()
 
     @pl.when(late)
     def _():
         spread_wait(2)
-        weight_grads(1)
-
-    near_copy(0, (1 - r) * nd + d).wait_recv()
+        dec_weight_grads()
+
+    near_copy(0, d * nr + 1 - r).wait_recv()
+    add_chip(0, d, True)
     for j in range(1, nd):
         relay_copy(j, 1 - r).wait_recv()
-    weight_grads(0)
+        add_chip(0, lax.rem(d - j + nd, nd), False)
+    write_grads(out_we)
     spread_wait(4)
     total = jnp.sum(gains[...], axis=0)
     width = out_ge.shape[1]
@@ -683,7 +721,7 @@
         hop(3, -1).wait_send()
 
     for j in range(nd):
-        near_copy(j, me).wait_send()
+        near_copy(j, slot).wait_send()
     for j in range(1, nd):
         relay_copy(j, r).wait_send()
 
@@ -712,8 +750,6 @@
         min((i * share + share - 1) // channels, 26) - i * share // channels + 1
         for i in range(peers)
     )
-    owner = np.arange(channels) // (channels // GROUPS)
-    groups = jnp.asarray(owner[:, None] == owner[None, :], BF16)
     field = pltpu.VMEM((cells, channels), BF16)
     wide = pltpu.VMEM((cells, channels), F32)
     weights = pltpu.VMEM((taps, channels), BF16)
@@ -722,6 +758,8 @@
     vector = pltpu.VMEM((1, channels), F32)
     vmem = pl.BlockSpec(memory_space=pltpu.VMEM)
     anywhere = pl.BlockSpec(memory_space=pl.ANY)
+    far = pl.BlockSpec(memory_space=pltpu.HBM)
+    part = pltpu.VMEM(latent.shape, BF16)
     dma = pltpu.SemaphoreType.DMA
     flops = 2 * cells * taps * channels * 4 + 4 * share * peers * cells * channels
     grads = jax.ShapeDtypeStruct((1, channels, share), F32)
@@ -730,9 +768,10 @@
     results = pl.pallas_call(
         functools.partial(level_kernel, (ns, nr, nd), float(counted), loss_scale, blocks),
         out_shape=shapes,
-        in_specs=[vmem, vmem, anywhere, anywhere, vmem, vmem, vmem],
+        in_specs=[far] * 6,
         out_specs=(vmem, vmem, vmem, vmem),
         scratch_shapes=[
+            part, part, vector, vector, pltpu.VMEM((channels, channels), BF16),
             turned, turned, weights, weights, weights, weights,
             pltpu.VMEM((2, cells // 2, channels), BF16),
             pltpu.VMEM((2, cells // 2, channels), BF16),
@@ -743,25 +782,26 @@
             pltpu.VMEM((blocks, channels, peers * cells), BF16),
             pltpu.VMEM((blocks, channels, peers * cells), BF16),
             pltpu.VMEM((blocks * channels, channels), F32),
-            dma((2,)), dma((4,)), dma((4,)), dma((2,)), dma((2,)),
+            dma((2,)), dma((4,)), dma((4,)), dma((4,)), dma((2,)), dma((2,)),
             dma((5, peers)), dma((5, peers)),
         ],
         compiler_params=pltpu.CompilerParams(
-            collective_id=0, has_side_effects=True, vmem_limit_bytes=48 * 1024 * 1024
+            collective_id=0, has_side_effects=True, vmem_limit_bytes=62 * 1024 * 1024
         ),
         cost_estimate=pl.CostEstimate(
             flops=flops, bytes_accessed=4 * taps * channels, transcendentals=4 * cells * channels
         ),
     )(
         latent, out_grad, jnp.swapaxes(enc_weight, 1, 2), jnp.swapaxes(dec_weight, 1, 2),
-        enc_gain, dec_gain, groups,
+        enc_gain, dec_gain,
     )
     enc, dec, enc_g, dec_g = pl.pallas_call(
         write_kernel,
         out_shape=shapes,
-        in_specs=[vmem] * 4,
+        in_specs=[anywhere] * 4,
         out_specs=(anywhere,) * 4,
         scratch_shapes=[dma((4,))],
+        compiler_params=pltpu.CompilerParams(vmem_limit_bytes=62 * 1024 * 1024),
     )(*results)
     return (jnp.swapaxes(enc, 1, 2), jnp.swapaxes(dec, 1, 2), enc_g, dec_g)
 

time: 86.1 us -> 112 us (1.30)
  Pallas kernels: 74.3 us -> 111 us
  local copies, waits for them, and re-layouts: 9.73 us -> 0 us
    pallas_call x1, Pallas kernels: 2.29 us -> 36.9 us  [one_kernel(): pl.pallas_call(write_kernel, out_shape=shapes, in_specs=[anywhere] * 4, o...]
    unnamed x22 -> x0, local copies, waits for them, and re-layouts: 9.73 us -> none
    pallas_call x1, Pallas kernels: 72 us -> 73.9 us  [one_kernel(): pl.pallas_call(functools.partial(level_kernel, (ns, nr, nd), float(counte...]
where the time goes in v3:
time: 112 us; the launch traced here: 111 us
  Pallas kernels  111 us (99%)
    pallas_call x1, Pallas kernels, one_kernel(): pl.pallas_call(functools.partial(level_kernel, (ns, nr, nd), float(counte...  73.9 us
    pallas_call x1, Pallas kernels, one_kernel(): pl.pallas_call(write_kernel, out_shape=shapes, in_specs=[anywhere] * 4, o...  36.9 us

profile of v3, /device:TPU:0, one launch (start us, length us, event | category | flops | bytes accessed | tf_op | source)
XLA Modules:
  0.0 111.5 jit_solution(3424693166515263895)
XLA Ops:
  0.6 73.9 %shard_map.93 = (f32[1,192,648]{2,1,0:T(8,128)}, f32[1,192,648]{2,1,0:T(8,128)}, f32[1,24]{1,0:T(1,128)}, f32[1,24]{1,0:T(1,128)}) custom-call(bf16[2,2,4,8,192]{4,3,2,1,0:T(8,128)(2,1)} %lat_hbm.1, bf16[2,2,4,8,192]{4,3,2,1,0:T(8,128)(2,1)} %grad_hbm.1, bf16[1,192,5184]{2,1,0:T(8,128)(2,1)} %bitcast.4, bf16[1,192,5184]{2,1,0:T(8,128)(2,1)} %bitcast.5, ...), custom_call_target="tpu_custom_call" | custom-call | flops 1528823808 | bytes 3981312 | tf_op jit(solution)/shard_map/pallas_call | solution.py:768
  74.6 36.9 %shard_map.94 = (f32[1,192,648]{2,1,0:T(8,128)}, f32[1,192,648]{2,1,0:T(8,128)}, f32[1,24]{1,0:T(1,128)}, f32[1,24]{1,0:T(1,128)}) custom-call(f32[1,192,648]{2,1,0:T(8,128)} %get-tuple-element.12.refs_0_, f32[1,192,648]{2,1,0:T(8,128)} %get-tuple-element.13.refs_1_, f32[1,24]{1,0:T(1,128)} %get-tuple-element.14.refs_2_, f32[1,24]{1,0:T(1,128)} %get-tuple-element.15.refs_3_), custom_call_target="tpu_custom_call" | custom-call | tf_op jit(solution)/shard_map/pallas_call | solution.py:798

commit v4 on v3

--- a/solution.py
+++ b/solution.py
@@ -727,13 +727,15 @@
 
 
 def write_kernel(*refs):
-    sources, targets, sems = refs[:4], refs[4:8], refs[8]
-    copies = [
-        pltpu.make_async_copy(a, b, sems.at[i]) for i, (a, b) in enumerate(zip(sources, targets))
-    ]
-    for c in copies:
+    sources, targets, held, sems = refs[:4], refs[4:8], refs[8:12], refs[12]
+    arrive = [pltpu.make_async_copy(sources[i], held[i], sems.at[0, i]) for i in range(4)]
+    leave = [pltpu.make_async_copy(held[i], targets[i], sems.at[1, i]) for i in range(4)]
+    for c in arrive:
         c.start()
-    for c in copies:
+    for c, after in zip(arrive, leave):
+        c.wait()
+        after.start()
+    for c in leave:
         c.wait()
 
 
@@ -800,7 +802,7 @@
         out_shape=shapes,
         in_specs=[anywhere] * 4,
         out_specs=(anywhere,) * 4,
-        scratch_shapes=[dma((4,))],
+        scratch_shapes=[pltpu.VMEM(x.shape, F32) for x in shapes] + [dma((2, 4))],
         compiler_params=pltpu.CompilerParams(vmem_limit_bytes=62 * 1024 * 1024),
     )(*results)
     return (jnp.swapaxes(enc, 1, 2), jnp.swapaxes(dec, 1, 2), enc_g, dec_g)

time: 112 us -> 77.3 us (0.69)
  Pallas kernels: 111 us -> 76.1 us
    pallas_call x1, Pallas kernels: 36.9 us -> 2.15 us  [one_kernel(): pl.pallas_call(write_kernel, out_shape=shapes, in_specs=[anywhere] * 4, o...]
where the time goes in v4:
time: 77.3 us; the launch traced here: 76.7 us
  Pallas kernels  76.1 us (98%)
    pallas_call x1, Pallas kernels, one_kernel(): pl.pallas_call(functools.partial(level_kernel, (ns, nr, nd), float(counte...  73.9 us
    pallas_call x1, Pallas kernels, one_kernel(): pl.pallas_call(write_kernel, out_shape=shapes, in_specs=[anywhere] * 4, o...  2.15 us

profile of v4, /device:TPU:0, one launch (start us, length us, event | category | flops | bytes accessed | tf_op | source)
XLA Modules:
  0.0 76.7 jit_solution(7448751909348479342)
XLA Ops:
  0.6 73.9 %shard_map.93 = (f32[1,192,648]{2,1,0:T(8,128)}, f32[1,192,648]{2,1,0:T(8,128)}, f32[1,24]{1,0:T(1,128)}, f32[1,24]{1,0:T(1,128)}) custom-call(bf16[2,2,4,8,192]{4,3,2,1,0:T(8,128)(2,1)} %lat_hbm.1, bf16[2,2,4,8,192]{4,3,2,1,0:T(8,128)(2,1)} %grad_hbm.1, bf16[1,192,5184]{2,1,0:T(8,128)(2,1)} %bitcast.4, bf16[1,192,5184]{2,1,0:T(8,128)(2,1)} %bitcast.5, ...), custom_call_target="tpu_custom_call" | custom-call | flops 1528823808 | bytes 3981312 | tf_op jit(solution)/shard_map/pallas_call | solution.py:770
  74.6 2.1 %shard_map.94 = (f32[1,192,648]{2,1,0:T(8,128)}, f32[1,192,648]{2,1,0:T(8,128)}, f32[1,24]{1,0:T(1,128)}, f32[1,24]{1,0:T(1,128)}) custom-call(f32[1,192,648]{2,1,0:T(8,128)} %get-tuple-element.12.refs_0_, f32[1,192,648]{2,1,0:T(8,128)} %get-tuple-element.13.refs_1_, f32[1,24]{1,0:T(1,128)} %get-tuple-element.14.refs_2_, f32[1,24]{1,0:T(1,128)} %get-tuple-element.15.refs_3_), custom_call_target="tpu_custom_call" | custom-call | tf_op jit(solution)/shard_map/pallas_call | solution.py:800
